TPU v7x, 32 devices: a whole 2x2x4 slice. The times are simulated.
32 devices in a mesh: dp: 4 (over z), ctx: 2 (over x), tensor: 4 (over y, core).
Axes of the slice: x: 2, y: 2, z: 4, core: 2. Of those that a mesh axis runs over, the one named last changes fastest.
Arguments:
- tokens: bfloat16 [4, 2048, 1024], P('dp', 'ctx'), may hold values from -6 to 6
- first_gain: float32 [1024], replicated, may hold values from 0.5 to 1.5
- query_weight: bfloat16 [1024, 1024], P(None, 'tensor'), may hold values from -0.1875 to 0.1875
- key_weight: bfloat16 [1024, 1024], P(None, 'tensor'), may hold values from -0.1875 to 0.1875
- value_weight: bfloat16 [1024, 2048], P(None, 'tensor'), may hold values from -0.1875 to 0.1875
- outgate_weight: bfloat16 [1024, 2048], P(None, 'tensor'), may hold values from -0.1875 to 0.1875
- alpha_weight: bfloat16 [1024, 8], P(None, 'tensor'), may hold values from -0.1875 to 0.1875
- beta_weight: bfloat16 [1024, 8], P(None, 'tensor'), may hold values from -0.1875 to 0.1875
- query_conv: float32 [4, 1024], P(None, 'tensor'), may hold values from -3 to 3
- convolved_keys: float32 [4, 1024], P(None, 'tensor'), may hold values from -3 to 3
- value_conv: float32 [4, 2048], P(None, 'tensor'), may hold values from -3 to 3
- decay_rate: float32 [8], P('tensor'), may hold values from 0.0002 to 0.08
- time_bias: float32 [8], P('tensor'), may hold values from -1 to 1
- head_gain: float32 [256], replicated, may hold values from 0.5 to 1.5
- out_weight: bfloat16 [2048, 1024], P('tensor'), may hold values from -0.25 to 0.25
- second_gain: float32 [1024], replicated, may hold values from 0.5 to 1.5
- gate_weight: bfloat16 [1024, 2816], P(None, 'tensor'), may hold values from -0.1875 to 0.1875
- up_weight: bfloat16 [1024, 2816], P(None, 'tensor'), may hold values from -0.1875 to 0.1875
- down_weight: bfloat16 [2816, 1024], P('tensor'), may hold values from -0.109375 to 0.109375
- cotangent: bfloat16 [4, 2048, 1024], P('dp', 'ctx'), may hold values from -6 to 6
Outputs:
- block_out: bfloat16 [4, 2048, 1024], P('dp', 'ctx')
- tokens_grad: bfloat16 [4, 2048, 1024], P('dp', 'ctx')
- first_gain_grad: float32 [1024], replicated
- query_weight_grad: float32 [1024, 1024], P(('dp', 'ctx'), 'tensor')
- key_weight_grad: float32 [1024, 1024], P(('dp', 'ctx'), 'tensor')
- value_weight_grad: float32 [1024, 2048], P(('dp', 'ctx'), 'tensor')
- outgate_weight_grad: float32 [1024, 2048], P(('dp', 'ctx'), 'tensor')
- alpha_weight_grad: float32 [1024, 8], P(('dp', 'ctx'), 'tensor')
- beta_weight_grad: float32 [1024, 8], P(('dp', 'ctx'), 'tensor')
- query_conv_grad: float32 [4, 1024], P(None, 'tensor')
- key_conv_grad: float32 [4, 1024], P(None, 'tensor')
- value_conv_grad: float32 [4, 2048], P(None, 'tensor')
- decay_rate_grad: float32 [8], P('tensor')
- time_bias_grad: float32 [8], P('tensor')
- head_gain_grad: float32 [256], replicated
- out_weight_grad: float32 [2048, 1024], P('tensor', ('dp', 'ctx'))
- second_gain_grad: float32 [1024], replicated
- gate_weight_grad: float32 [1024, 2816], P(('dp', 'ctx'), 'tensor')
- up_weight_grad: float32 [1024, 2816], P(('dp', 'ctx'), 'tensor')
- down_weight_grad: float32 [2816, 1024], P('tensor', ('dp', 'ctx'))
All inputs are finite; a program needn't handle non-finite values.
Results may differ from a plain program's by a relative error of at most 0.038.
Values may be sent and summed in bfloat16 or wider, within the bound.
A program may use at most 192 MiB of HBM per device.

v0:
```python
import jax
import jax.numpy as jnp
from jax import lax
from jax.sharding import PartitionSpec as P

KCONV = 4
SPAN = 64


epsilon = 1e-06
maximal_precision = lax.Precision.HIGHEST


def shifted(value, axis, by):
    devices = lax.axis_size(axis)
    pairs = [(i, i + by) for i in range(devices) if 0 <= i + by < devices]
    return lax.ppermute(value, axis, pairs)


def entering(value, axis, combine, identity, reverse):
    devices, index = (lax.axis_size(axis), lax.axis_index(axis))
    everything = jax.tree.map(
        lambda part, kind: lax.all_gather(part.astype(kind), axis),
        value,
        (jnp.bfloat16, jnp.bfloat16),
    )
    start = jax.tree.map(
        lambda part, zero: jnp.broadcast_to(jnp.asarray(zero, part.dtype), part.shape),
        value,
        identity,
    )

    def lap(k, before):
        at = devices - 1 - k if reverse else k
        reached = at > index if reverse else at < index
        new = combine(
            before, jax.tree.map(lambda part, own: part[at].astype(own.dtype), everything, value)
        )
        return jax.tree.map(lambda a, b: jnp.where(reached, a, b), new, before)

    return lax.fori_loop(0, devices, lap, start)


def high_dot(left, right):
    return jnp.matmul(left, right, precision=maximal_precision)


def flipped(matrix):
    return jnp.swapaxes(matrix, -1, -2)


def span_first(array_in):
    return jnp.moveaxis(array_in, 1, 0)


def rms_gain(rows_in, gain_in):
    return rows_in * lax.rsqrt(jnp.mean(rows_in * rows_in, -1, keepdims=True) + epsilon) * gain_in


def gated_out(head_vals, gate_vals, gain_in):
    return rms_gain(head_vals, gain_in) * jax.nn.silu(gate_vals)


def swiglu(gate_in, up_in):
    return jax.nn.silu(gate_in) * up_in


def span_maps(queries, keys_in, values_in, log_gate, strength):
    block_len = log_gate.shape[-1]
    key_dim = keys_in.shape[-1]
    cumulated = jnp.cumsum(log_gate, -1)
    row_index = jnp.arange(block_len)[:, None]
    col_index = jnp.arange(block_len)[None, :]
    causal = row_index >= col_index
    strictly = row_index > col_index
    log_ratio = cumulated[..., :, None] - cumulated[..., None, :]
    decays = jnp.where(causal, jnp.exp(jnp.where(causal, log_ratio, 0.0)), 0.0)
    keys_flip = flipped(keys_in)
    lower_part = (
        jnp.where(strictly, decays * high_dot(keys_in, keys_flip), 0.0) * strength[..., :, None]
    )
    unit_lower = lower_part + jnp.eye(block_len, dtype=jnp.float32)
    gammas = jnp.exp(cumulated)
    right_side = jnp.concatenate(
        [(strength * gammas)[..., None] * keys_in, strength[..., None] * values_in], -1
    )
    solved = lax.linalg.triangular_solve(
        unit_lower, right_side, left_side=True, lower=True, unit_diagonal=True
    )
    key_solve = solved[..., :key_dim]
    value_solve = solved[..., key_dim:]
    mixing = decays * high_dot(queries, keys_flip)
    emitted = gammas[..., None] * queries - high_dot(mixing, key_solve)
    offsets = high_dot(mixing, value_solve)
    tail_keys = flipped(jnp.exp(cumulated[..., -1:] - cumulated)[..., None] * keys_in)
    carry_map = gammas[..., -1, None, None] * jnp.eye(key_dim, dtype=jnp.float32) - high_dot(
        tail_keys, key_solve
    )
    carry_add = high_dot(tail_keys, value_solve)
    return (emitted, offsets, carry_map, carry_add)


def run_spans(emitted, offsets, carry_map, carry_add, state_in):

    def advance(recurrent_state, pieces):
        emit_now, offset_now, map_now, add_now = pieces
        return (
            high_dot(map_now, recurrent_state) + add_now,
            high_dot(emit_now, recurrent_state) + offset_now,
        )

    state_out, outputs = lax.scan(
        advance,
        state_in,
        (span_first(emitted), span_first(offsets), span_first(carry_map), span_first(carry_add)),
    )
    return (span_first(outputs), state_out)


def combine_maps(earlier, later):
    return (high_dot(later[0], earlier[0]), high_dot(later[0], earlier[1]) + later[1])


def identity_maps(carry_map, carry_add):
    lane_count = carry_map.shape[0]
    key_dim = carry_map.shape[-1]
    eye_block = jnp.broadcast_to(
        jnp.eye(key_dim, dtype=jnp.float32), (lane_count, key_dim, key_dim)
    )
    return (eye_block, jnp.zeros((lane_count,) + carry_add.shape[-2:], jnp.float32))


def compose_maps(carry_map, carry_add):

    def absorb(total, pieces):
        return (combine_maps(total, pieces), None)

    result, unused = lax.scan(
        absorb, identity_maps(carry_map, carry_add), (span_first(carry_map), span_first(carry_add))
    )
    return result


def state_pull(emitted, carry_map, out_grad):
    initial = jnp.zeros(emitted.shape[:1] + (emitted.shape[-1], out_grad.shape[-1]), jnp.float32)

    def retreat(total, pieces):
        emit_now, map_now, grad_now = pieces
        return (high_dot(flipped(map_now), total) + high_dot(flipped(emit_now), grad_now), None)

    pulled, unused = lax.scan(
        retreat,
        initial,
        (span_first(emitted), span_first(carry_map), span_first(out_grad)),
        reverse=True,
    )
    return pulled


def per_device(
    tokens,
    first_gain,
    query_weight,
    key_weight,
    value_weight,
    outgate_weight,
    alpha_weight,
    beta_weight,
    query_conv,
    convolved_keys,
    value_conv,
    decay_rate,
    time_bias,
    head_gain,
    out_weight,
    second_gain,
    gate_weight,
    up_weight,
    down_weight,
    cotangent,
):
    seq_count, local_len, model_width = tokens.shape
    rows = seq_count * local_len
    heads = decay_rate.shape[0]
    q_cols = query_weight.shape[1]
    k_cols = key_weight.shape[1]
    v_cols = value_weight.shape[1]
    key_dim = q_cols // heads
    val_dim = v_cols // heads
    spans = local_len // SPAN
    lane_count = seq_count * heads

    def to_spans(block_in):
        return jnp.transpose(block_in, (0, 2, 1, 3)).reshape(
            lane_count, spans, SPAN, block_in.shape[-1]
        )

    def to_lanes(block_in):
        return jnp.transpose(block_in, (0, 2, 1)).reshape(lane_count, spans, SPAN)

    def rounded(values_f):
        return lax.optimization_barrier(values_f.astype(jnp.bfloat16)).astype(jnp.float32)

    def mixer_front(padded_in, kernel_in, alpha_in, beta_in, decay_in, bias_in):
        summed = sum(
            (
                kernel_in[tap_index] * padded_in[:, tap_index : tap_index + local_len, :]
                for tap_index in range(KCONV)
            )
        )
        active = jax.nn.silu(summed)
        raw_query = active[..., :q_cols].reshape(seq_count, local_len, heads, key_dim)
        raw_key = active[..., q_cols : q_cols + k_cols].reshape(
            seq_count, local_len, heads, key_dim
        )
        raw_value = active[..., q_cols + k_cols :].reshape(seq_count, local_len, heads, val_dim)
        unit_query = (
            raw_query
            * lax.rsqrt(jnp.sum(raw_query * raw_query, -1, keepdims=True) + epsilon)
            * key_dim ** (-0.5)
        )
        unit_key = raw_key * lax.rsqrt(jnp.sum(raw_key * raw_key, -1, keepdims=True) + epsilon)
        log_gate = -decay_in * jax.nn.softplus(
            alpha_in.reshape(seq_count, local_len, heads) + bias_in
        )
        strength = jax.nn.sigmoid(beta_in.reshape(seq_count, local_len, heads))
        return (
            to_spans(unit_query),
            to_spans(unit_key),
            to_spans(raw_value),
            to_lanes(log_gate),
            to_lanes(strength),
        )

    inputs = tokens.reshape(rows, model_width).astype(jnp.float32)
    normed1, norm1_back = jax.vjp(rms_gain, inputs, first_gain)
    normed1_b = normed1.astype(jnp.bfloat16)

    def project(weight):
        return jnp.dot(normed1_b, weight, preferred_element_type=jnp.float32)

    linear = jnp.concatenate([project(query_weight), project(key_weight), project(value_weight)], 1)
    linear = linear.astype(jnp.bfloat16).reshape(seq_count, local_len, q_cols + k_cols + v_cols)
    gate_lin = project(outgate_weight)
    alpha_lin = project(alpha_weight)
    beta_lin = project(beta_weight)
    rims = shifted(linear[:, local_len - (KCONV - 1) :, :], "ctx", 1)
    padded = jnp.concatenate([rims, linear], 1).astype(jnp.float32)
    kernel = jnp.concatenate([query_conv, convolved_keys, value_conv], 1)
    front_out, front_back = jax.vjp(
        mixer_front, padded, kernel, alpha_lin, beta_lin, decay_rate, time_bias
    )
    queries = rounded(front_out[0])
    keys_in = rounded(front_out[1])
    values_in = rounded(front_out[2])
    maps_out, maps_back = jax.vjp(
        span_maps, queries, keys_in, values_in, front_out[3], front_out[4]
    )
    device_map, device_add = compose_maps(maps_out[2], maps_out[3])
    prefix = entering(
        (device_map, device_add), "ctx", combine_maps, identity_maps(device_map, device_add), False
    )
    state_in = prefix[1]
    (head_spans, state_end), run_back = jax.vjp(
        run_spans, maps_out[0], maps_out[1], maps_out[2], maps_out[3], state_in
    )
    head_out = jnp.transpose(
        head_spans.reshape(seq_count, heads, local_len, head_spans.shape[-1]), (0, 2, 1, 3)
    )
    gate_heads = gate_lin.reshape(seq_count, local_len, heads, val_dim)
    normed_heads, gated_back = jax.vjp(gated_out, head_out, gate_heads, head_gain)
    normed_heads_b = normed_heads.reshape(rows, v_cols).astype(jnp.bfloat16)
    mixer_part = jnp.dot(normed_heads_b, out_weight, preferred_element_type=jnp.float32)
    middle = inputs + lax.psum(mixer_part.astype(jnp.bfloat16), "tensor").astype(jnp.float32)
    normed2, second_norm_backward = jax.vjp(rms_gain, middle, second_gain)
    normed2_b = normed2.astype(jnp.bfloat16)
    gate_pre = jnp.dot(normed2_b, gate_weight, preferred_element_type=jnp.float32)
    up_pre = jnp.dot(normed2_b, up_weight, preferred_element_type=jnp.float32)
    hidden_f, swiglu_back = jax.vjp(swiglu, gate_pre, up_pre)
    hidden = hidden_f.astype(jnp.bfloat16)
    ffn_part = jnp.dot(hidden, down_weight, preferred_element_type=jnp.float32)
    block_out = (
        middle + lax.psum(ffn_part.astype(jnp.bfloat16), "tensor").astype(jnp.float32)
    ).astype(jnp.bfloat16)
    grad_rows = cotangent.reshape(rows, model_width)
    down_grad_w = jnp.dot(hidden.T, grad_rows, preferred_element_type=jnp.float32)
    hidden_grad = jnp.dot(grad_rows, down_weight.T, preferred_element_type=jnp.float32)
    gate_grad, up_grad = swiglu_back(hidden_grad)
    gate_grad_b = gate_grad.astype(jnp.bfloat16)
    up_grad_b = up_grad.astype(jnp.bfloat16)
    gate_grad_w = jnp.dot(normed2_b.T, gate_grad_b, preferred_element_type=jnp.float32)
    up_grad_w = jnp.dot(normed2_b.T, up_grad_b, preferred_element_type=jnp.float32)
    normed2_part = jnp.dot(gate_grad_b, gate_weight.T, preferred_element_type=jnp.float32)
    normed2_part = normed2_part + jnp.dot(
        up_grad_b, up_weight.T, preferred_element_type=jnp.float32
    )
    normed2_grad = lax.psum(normed2_part.astype(jnp.bfloat16), "tensor").astype(jnp.float32)
    middle_norm_grad, second_gain_grad = second_norm_backward(normed2_grad)
    middle_grad = grad_rows.astype(jnp.float32) + middle_norm_grad
    middle_low = middle_grad.astype(jnp.bfloat16)
    out_grad_w = jnp.dot(normed_heads_b.T, middle_low, preferred_element_type=jnp.float32)
    heads_grad = jnp.dot(middle_low, out_weight.T, preferred_element_type=jnp.float32).reshape(
        seq_count, local_len, heads, val_dim
    )
    head_out_grad, head_gate_gradient, head_gain_grad = gated_back(heads_grad)
    out_spans_grad = to_spans(head_out_grad)
    local_pull = state_pull(maps_out[0], maps_out[2], out_spans_grad)
    suffix = entering(
        (flipped(device_map), local_pull),
        "ctx",
        combine_maps,
        identity_maps(device_map, device_add),
        True,
    )
    emitted_grad, offsets_grad, map_grad, add_grad, state_in_grad = run_back(
        (out_spans_grad, suffix[1])
    )
    query_grad, key_grad, value_grad, log_gate_grad, strength_grad = maps_back(
        (emitted_grad, offsets_grad, map_grad, add_grad)
    )
    padded_grad, kernel_grad, alpha_grad, beta_grad, decay_grad, bias_grad = front_back(
        (query_grad, key_grad, value_grad, log_gate_grad, strength_grad)
    )
    rim_back = shifted(padded_grad[:, : KCONV - 1, :].astype(jnp.bfloat16), "ctx", -1).astype(
        jnp.float32
    )
    linear_grad = padded_grad[:, KCONV - 1 :, :] + jnp.pad(
        rim_back, ((0, 0), (local_len - (KCONV - 1), 0), (0, 0))
    )
    linear_grad_b = linear_grad.reshape(rows, q_cols + k_cols + v_cols).astype(jnp.bfloat16)
    query_lin_grad = linear_grad_b[:, :q_cols]
    key_lin_grad = linear_grad_b[:, q_cols : q_cols + k_cols]
    value_lin_grad = linear_grad_b[:, q_cols + k_cols :]
    gate_lin_grad = head_gate_gradient.reshape(rows, v_cols).astype(jnp.bfloat16)
    alpha_lin_grad = alpha_grad.astype(jnp.bfloat16)
    beta_lin_grad = beta_grad.astype(jnp.bfloat16)
    paired = (
        (query_weight, query_lin_grad),
        (key_weight, key_lin_grad),
        (value_weight, value_lin_grad),
        (outgate_weight, gate_lin_grad),
        (alpha_weight, alpha_lin_grad),
        (beta_weight, beta_lin_grad),
    )
    normed1_part = sum(
        (jnp.dot(grad_b, weight.T, preferred_element_type=jnp.float32) for weight, grad_b in paired)
    )
    mixer_w = [
        jnp.dot(normed1_b.T, grad_b, preferred_element_type=jnp.float32)
        for weight, grad_b in paired
    ]
    tensor_terms = (normed1_part, head_gain_grad)
    tensor_sums = (
        lax.psum(tensor_terms[0].astype(jnp.bfloat16), "tensor").astype(jnp.float32),
        lax.psum(tensor_terms[1].astype(jnp.bfloat16), "tensor").astype(jnp.float32),
    )
    normed1_grad = tensor_sums[0]
    head_gain_total = tensor_sums[1]
    inputs_norm_grad, first_gain_grad = norm1_back(normed1_grad)
    tokens_grad = (middle_grad + inputs_norm_grad).astype(jnp.bfloat16)
    weight_grads = (
        lax.psum_scatter(mixer_w[0], ("dp", "ctx"), scatter_dimension=0, tiled=True),
        lax.psum_scatter(mixer_w[1], ("dp", "ctx"), scatter_dimension=0, tiled=True),
        lax.psum_scatter(mixer_w[2], ("dp", "ctx"), scatter_dimension=0, tiled=True),
        lax.psum_scatter(mixer_w[3], ("dp", "ctx"), scatter_dimension=0, tiled=True),
        lax.psum_scatter(mixer_w[4], ("dp", "ctx"), scatter_dimension=0, tiled=True),
        lax.psum_scatter(mixer_w[5], ("dp", "ctx"), scatter_dimension=0, tiled=True),
        lax.psum_scatter(out_grad_w, ("dp", "ctx"), scatter_dimension=1, tiled=True),
        lax.psum_scatter(gate_grad_w, ("dp", "ctx"), scatter_dimension=0, tiled=True),
        lax.psum_scatter(up_grad_w, ("dp", "ctx"), scatter_dimension=0, tiled=True),
        lax.psum_scatter(down_grad_w, ("dp", "ctx"), scatter_dimension=1, tiled=True),
    )
    small_sums = lax.psum(
        (first_gain_grad, second_gain_grad, head_gain_total, kernel_grad, decay_grad, bias_grad),
        ("dp", "ctx"),
    )
    kernel_sum = small_sums[3]
    return (
        block_out.reshape(seq_count, local_len, model_width),
        tokens_grad.reshape(seq_count, local_len, model_width),
        small_sums[0],
        weight_grads[0],
        weight_grads[1],
        weight_grads[2],
        weight_grads[3],
        weight_grads[4],
        weight_grads[5],
        kernel_sum[:, :q_cols],
        kernel_sum[:, q_cols : q_cols + k_cols],
        kernel_sum[:, q_cols + k_cols :],
        small_sums[4],
        small_sums[5],
        small_sums[2],
        weight_grads[6],
        small_sums[1],
        weight_grads[7],
        weight_grads[8],
        weight_grads[9],
    )


def solution(mesh):
    placed = (
        P("dp", "ctx", None),
        P(),
        P(None, "tensor"),
        P(None, "tensor"),
        P(None, "tensor"),
        P(None, "tensor"),
        P(None, "tensor"),
        P(None, "tensor"),
        P(None, "tensor"),
        P(None, "tensor"),
        P(None, "tensor"),
        P("tensor"),
        P("tensor"),
        P(),
        P("tensor", None),
        P(),
        P(None, "tensor"),
        P(None, "tensor"),
        P("tensor", None),
        P("dp", "ctx", None),
    )
    return jax.shard_map(
        per_device,
        mesh=mesh,
        in_specs=placed,
        out_specs=(
            P("dp", "ctx", None),
            P("dp", "ctx", None),
            P(),
            P(("dp", "ctx"), "tensor"),
            P(("dp", "ctx"), "tensor"),
            P(("dp", "ctx"), "tensor"),
            P(("dp", "ctx"), "tensor"),
            P(("dp", "ctx"), "tensor"),
            P(("dp", "ctx"), "tensor"),
            P(None, "tensor"),
            P(None, "tensor"),
            P(None, "tensor"),
            P("tensor"),
            P("tensor"),
            P(),
            P("tensor", ("dp", "ctx")),
            P(),
            P(("dp", "ctx"), "tensor"),
            P(("dp", "ctx"), "tensor"),
            P("tensor", ("dp", "ctx")),
        ),
        check_vma=False,
    )
```

profile of v0, /device:TPU:0, one launch (start us, length us, event | category | flops | bytes accessed | tf_op | source)
XLA Modules:
  0.0 1673.1 jit_solution(3355062584464821680)
XLA Ops:
  15.9 5.7 collective-permute-start
  35.1 4.5 fusion.282
  45.9 5.4 fusion.90
  71.8 158.9 %custom-call.7 = f32[2,16,1,64,64]{3,4,2,1,0:T(8,128)} custom-call(f32[2,16,1,64,64]{4,3,2,1,0:T(8,128)} %add_bitcast_fusion), custom_call_target="InvertDiagBlocksLowerTriangular" | custom-call | tf_op jit(solution)/shard_map/jvp()/triangular_solve | solution.py:87
  232.2 5.0 fusion.95
  257.8 92.6 %while.96 = (s32[]{:T(128)}, f32[2,128,128]{2,1,0:T(8,128)}, f32[2,128,256]{2,1,0:T(8,128)}, f32[16,2,128,128]{3,2,1,0:T(8,128)}, f32[16,2,128,256]{3,2,1,0:T(8,128)}, /*index=5*/s32[]{:T(128)}, s32[]{:T(128)}) while((s32[]{:T(128)}, f32[2,128,128]{2,1,0:T(8,128)}, f32[2,128,256]{2,1,0:T(8,128)}, f32[16,2,128,128]{3,2,1,0:T(8,128)}, ...), condition=%wide.region_4.5_spmd.clone, body=%wide.region_3.4_spmd.clone.sunk | while | flops 151126016 | bytes 2098786 | solution.py:138
  352.3 5.0 all-gather
  357.3 5.7 all-gather.1
  363.1 5.8 while.97
  371.3 90.2 %while.94 = (s32[]{:T(128)}, f32[2,128,256]{2,1,0:T(8,128)}, f32[16,2,64,256]{3,2,0,1:T(8,128)}, f32[16,2,128,256]{3,2,1,0:T(8,128)}, f32[16,2,128,128]{3,2,1,0:...) while((s32[]{:T(128)}, f32[2,128,256]{2,1,0:T(8,128)}, ...), condition=%wide.region_9.10_spmd, body=%wide.region_8.9_spmd.sunk | while | flops 151093248 | bytes 2558057 | solution.py:112
  474.8 51.6 %all-reduce.22.cloned.1.call-done = bf16[1024,1024]{1,0:T(8,128)(2,1)} async-done(((bf16[1024,1024]{1,0:T(8,128)(2,1)}), bf16[1024,1024]{1,0:T(8,128)(2,1)}) %all-reduce.22.cloned.1.call-update) | async-done | bytes 2097168 | tf_op jit(solution)/shard_map/psum | solution.py:274
  550.0 6.3 all-gather.2
  556.3 4.5 convolution_convert_fusion.1
  560.9 34.6 %all-reduce.24.cloned.1.call-done = bf16[1024,1024]{1,0:T(8,128)(2,1)} async-done(((bf16[1024,1024]{1,0:T(8,128)(2,1)}), bf16[1024,1024]{1,0:T(8,128)(2,1)}) %all-reduce.24.cloned.1.call-update) | async-done | bytes 2097168 | tf_op jit(solution)/shard_map/psum | solution.py:297
  595.5 4.7 fusion.78
  600.3 4.9 fusion.171
  608.3 4.7 multiply_reduce_fusion.5
  615.2 41.3 %while.98 = (s32[]{:T(128)}, f32[2,128,256]{2,1,0:T(8,128)S(1)}, f32[16,2,128,128]{2,3,1,0:T(8,128)}, f32[16,2,64,128]{3,2,1,0:T(8,128)}, f32[16,2,64,256]{3,2,1...) while((s32[]{:T(128)}, f32[2,128,256]{2,1,0:T(8,128)S(1)}, f32[16,2,128,128]{2,3,1,0:T(8,128)}, ...), condition=%wide.region_18.19_spmd.clone, body=%wide.region_17.18_spmd.clone.sunk | while | flops 151126016 | bytes 1377399 | solution.py:151
  656.5 6.3 all-gather.3
  667.9 124.1 %while.95 = (s32[]{:T(128)}, f32[2,128,256]{2,1,0:T(8,128)S(1)}, f32[16,2,64,128]{3,2,0,1:T(8,128)S(1)}, f32[16,2,64,256]{3,2,1,0:T(8,128)}, f32[16,2,128,128]{2...) while((s32[]{:T(128)}, f32[2,128,256]{2,1,0:T(8,128)S(1)}, ...), condition=%wide.region_22.23_spmd, body=%wide.region_21.22_spmd.sunk | while | flops 302055424 | bytes 3804813 | solution.py:112
  800.7 4.7 fusion.121
  811.6 5.5 fusion.151
  826.3 4.5 fusion.104
  845.3 7.1 fusion.161
  876.3 4.6 fusion.286
  886.5 6.2 multiply_reduce_fusion.3
  892.7 6.5 broadcast_multiply_fusion
  899.2 9.8 pad_add_fusion
  914.6 5.9 collective-permute-done.1
  928.5 5.8 add_convert_fusion
  941.5 6.3 fusion.169
  952.0 4.5 fusion.179
  956.5 5.2 fusion.113
  962.1 5.3 fusion.288
  967.5 5.3 fusion.287
  973.5 5.6 psum.85
  980.7 22.3 %reduce-scatter.31.cloned.1.call-done = f32[128,2]{1,0:T(8,128)} async-done(((f32[1024,2]{1,0:T(8,128)}), f32[128,2]{1,0:T(8,128)}) %reduce-scatter.31.cloned.1.call-update) | async-done | bytes 1040
  1004.4 86.1 %all-reduce.26.cloned.1.call-done = (bf16[1024,1024]{1,0:T(8,128)(2,1)}, bf16[1024,1024]{1,0:T(8,128)(2,1)}) async-done(((bf16[1024,1024]{1,0:T(8,128)(2,1)}, bf16[1024,1024]{1,0:T(8,128)(2,1)}), (bf16[1024,1024]{1,0:T(8,128)(2,1)}, bf16[1024,1024]{1,0:T(8,128)(2,1)})) %all-reduce.26.cloned.1.call-update) | async-done | bytes 4194320 | tf_op jit(solution)/shard_map/psum | solution.py:283
  1093.8 37.8 %all-reduce.16 = (f32[1024]{0:T(1024)}, f32[4,1024]{1,0:T(4,128)S(1)}, f32[2]{0:T(128)}, f32[2]{0:T(128)}, f32[256]{0:T(256)}, /*index=5*/f32[1024]{0:T(1024)}) all-reduce(f32[1024]{0:T(1024)S(1)} %get-tuple-element.824, f32[4,1024]{1,0:T(4,128)S(1)} %pad_add_fusion.4, ...), channel_id=1, replica_groups=mesh['dp'=4,'ctx'=2,'tensor'=4] {'dp','ctx'}, use_global_device_ids=true, to_apply=%region_38.39 | all-reduce | flops 6404 | bytes 50720 | tf_op jit(solution)/shard_map/psum | solution.py:373
  1132.9 7.1 fusion.111
  1140.0 18.3 %reduce-scatter.15.cloned.1.call-done = f32[128,256]{1,0:T(8,128)} async-done(((f32[1024,256]{1,0:T(8,128)}), f32[128,256]{1,0:T(8,128)}) %reduce-scatter.15.cloned.1.call-update) | async-done | bytes 131088 | tf_op jit(solution)/shard_map/reduce_scatter | solution.py:362
  1158.4 66.3 %reduce-scatter.17.cloned.1.call-done = f32[128,256]{1,0:T(8,128)} async-done(((f32[1024,256]{1,0:T(8,128)}), f32[128,256]{1,0:T(8,128)}) %reduce-scatter.17.cloned.1.call-update) | async-done | bytes 131088 | tf_op jit(solution)/shard_map/reduce_scatter | solution.py:363
  1224.7 71.8 %reduce-scatter.23.cloned.1.call-done = f32[512,128]{1,0:T(8,128)} async-done(((f32[512,1024]{1,0:T(8,128)}), f32[512,128]{1,0:T(8,128)}) %reduce-scatter.23.cloned.1.call-update) | async-done | bytes 262160 | tf_op jit(solution)/shard_map/reduce_scatter | solution.py:368
  1296.6 71.2 %reduce-scatter.21.cloned.1.call-done = f32[128,512]{1,0:T(8,128)} async-done(((f32[1024,512]{1,0:T(8,128)}), f32[128,512]{1,0:T(8,128)}) %reduce-scatter.21.cloned.1.call-update) | async-done | bytes 262160 | tf_op jit(solution)/shard_map/reduce_scatter | solution.py:365
  1367.7 71.0 %reduce-scatter.19.cloned.1.call-done = f32[128,512]{1,0:T(8,128)} async-done(((f32[1024,512]{1,0:T(8,128)}), f32[128,512]{1,0:T(8,128)}) %reduce-scatter.19.cloned.1.call-update) | async-done | bytes 262160 | tf_op jit(solution)/shard_map/reduce_scatter | solution.py:364
  1438.7 75.8 %reduce-scatter.29.cloned.1.call-done = f32[704,128]{1,0:T(8,128)} async-done(((f32[704,1024]{1,0:T(8,128)}), f32[704,128]{1,0:T(8,128)}) %reduce-scatter.29.cloned.1.call-update) | async-done | bytes 360464 | tf_op jit(solution)/shard_map/reduce_scatter | solution.py:371
  1514.5 75.8 %reduce-scatter.27.cloned.1.call-done = f32[128,704]{0,1:T(8,128)} async-done(((f32[1024,704]{0,1:T(8,128)}), f32[128,704]{0,1:T(8,128)}) %reduce-scatter.27.cloned.1.call-update) | async-done | bytes 360464 | tf_op jit(solution)/shard_map/reduce_scatter | solution.py:370
  1590.4 75.9 %reduce-scatter.25.cloned.1.call-done = f32[128,704]{0,1:T(8,128)} async-done(((f32[1024,704]{0,1:T(8,128)}), f32[128,704]{0,1:T(8,128)}) %reduce-scatter.25.cloned.1.call-update) | async-done | bytes 360464 | tf_op jit(solution)/shard_map/reduce_scatter | solution.py:369
  (760 shorter events, 576.0 us)
Async XLA Ops:
  7.2 527.5 %copy-start = (bf16[704,1024]{1,0:T(8,128)(2,1)S(1)}, bf16[704,1024]{1,0:T(8,128)(2,1)}, u32[]{:S(2)}) copy-start(bf16[704,1024]{1,0:T(8,128)(2,1)} %param.50) | copy-start | bytes 4325380
  7.2 519.2 %all-reduce.22.cloned.1.call-start = ((), (), s32[]{:S(2)}) async-start(), calls=%async_computation.10 | async-start | bytes 4194304 | tf_op jit(solution)/shard_map/psum | solution.py:274
  11.2 15.9 copy-start.31
  15.9 27.1 %collective-permute-start = (bf16[1,3,1024]{1,2,0:T(8,128)(2,1)}, bf16[1,3,1024]{1,2,0:T(8,128)(2,1)}, u32[]{:S(2)}, u32[]{:S(2)}) collective-permute-start(bf16[1,3,1024]{1,2,0:T(8,128)(2,1)} %pad_maximum_fusion), channel_id=1, source_target_pairs={{0,4},{1,5},{2,6},{3,7},{8,12},{9,13},{10,14},{11,15},{16,20},{17,... | collective-permute-start | bytes 18440 | tf_op jit(solution)/shard_map/ppermute | solution.py:17
  45.8 5.5 copy-start.2
  56.5 5.1 copy-start.25
  232.2 5.0 copy-start.12
  232.2 5.0 copy-start.41
  237.2 10.3 copy-start.3
  474.6 120.9 %all-reduce.24.cloned.1.call-start = ((), (), s32[]{:S(2)}) async-start(), calls=%async_computation.11 | async-start | bytes 4194304 | tf_op jit(solution)/shard_map/psum | solution.py:297
  543.9 435.3 %reduce-scatter.33.cloned.1.call-start = ((), (), s32[]{:S(2)}) async-start(), calls=%async_computation.21 | async-start | bytes 589824
  560.9 39.4 %copy-start.118 = (f32[1024]{0:T(1024)S(1)}, f32[1024]{0:T(1024)}, u32[]{:S(2)}) copy-start(f32[1024]{0:T(1024)} %copy-done.117) | copy-start | bytes 12292
  560.9 39.4 %copy-start.107 = (f32[1024]{0:T(1024)S(1)}, f32[1024]{0:T(1024)}, u32[]{:S(2)}) copy-start(f32[1024]{0:T(1024)} %copy-done.106) | copy-start | bytes 12292
  560.9 39.4 %copy-start.113 = (f32[1024]{0:T(1024)S(1)}, f32[1024]{0:T(1024)}, u32[]{:S(2)}) copy-start(f32[1024]{0:T(1024)} %param.47) | copy-start | bytes 12292
  615.2 47.6 %copy-start.29 = (f32[2,128,256]{2,1,0:T(8,128)S(1)}, f32[2,128,256]{2,1,0:T(8,128)}, u32[]{:S(2)}) copy-start(f32[2,128,256]{2,1,0:T(8,128)} %custom-call.11) | copy-start | bytes 786436
  615.2 47.6 %copy-start.64 = (bf16[4,128,128]{2,1,0:T(8,128)(2,1)S(1)}, bf16[4,128,128]{2,1,0:T(8,128)(2,1)}, u32[]{:S(2)}) copy-start(bf16[4,128,128]{2,1,0:T(8,128)(2,1)} %all-gather.2) | copy-start | bytes 393220
  656.5 7.0 copy-start.43
  667.9 128.4 %copy-start.78 = (pred[64,64]{1,0:T(8,128)(4,1)S(1)}, pred[64,64]{1,0:T(8,128)(4,1)}, u32[]{:S(2)}) copy-start(pred[64,64]{1,0:T(8,128)(4,1)} %get-tuple-element.957) | copy-start | bytes 12292
  794.4 6.3 copy-start.4
  811.6 5.6 copy-start.14
  811.6 5.6 copy-start.30
  845.2 7.2 copy-start.57
  845.2 7.9 copy-start.93
  845.2 7.9 copy-start.110
  845.2 7.9 copy-start.120
  876.0 126.9 %reduce-scatter.31.cloned.1.call-start = ((), (), s32[]{:S(2)}) async-start(), calls=%async_computation.20 | async-start | bytes 589824
  876.2 7.4 copy-start.26
  876.2 7.9 slice-start
  886.5 6.2 copy-start.123
  886.5 6.2 copy-start.125
  886.5 6.2 copy-start.127
  886.5 6.2 copy-start.129
  899.2 13.3 copy-start.6
  899.2 13.3 copy-start.111
  899.2 13.3 copy-start.121
  911.2 9.3 collective-permute-start.1
  914.3 9.3 copy-start.80
  914.3 176.1 %all-reduce.26.cloned.1.call-start = ((), (), s32[]{:S(2)}) async-start(), calls=%async_computation.22 | async-start | bytes 8388608 | tf_op jit(solution)/shard_map/psum | solution.py:283
  934.3 224.1 %reduce-scatter.15.cloned.1.call-start = ((), (), s32[]{:S(2)}) async-start(), calls=%async_computation.12 | async-start | bytes 1179648 | tf_op jit(solution)/shard_map/reduce_scatter | solution.py:362
  937.8 286.9 %reduce-scatter.17.cloned.1.call-start = ((), (), s32[]{:S(2)}) async-start(), calls=%async_computation.13 | async-start | bytes 1179648 | tf_op jit(solution)/shard_map/reduce_scatter | solution.py:363
  941.4 355.2 %reduce-scatter.23.cloned.1.call-start = ((), (), s32[]{:S(2)}) async-start(), calls=%async_computation.16 | async-start | bytes 2359296 | tf_op jit(solution)/shard_map/reduce_scatter | solution.py:368
  947.8 419.9 %reduce-scatter.21.cloned.1.call-start = ((), (), s32[]{:S(2)}) async-start(), calls=%async_computation.15 | async-start | bytes 2359296 | tf_op jit(solution)/shard_map/reduce_scatter | solution.py:365
  951.9 486.8 %reduce-scatter.19.cloned.1.call-start = ((), (), s32[]{:S(2)}) async-start(), calls=%async_computation.14 | async-start | bytes 2359296 | tf_op jit(solution)/shard_map/reduce_scatter | solution.py:364
  956.5 558.1 %reduce-scatter.29.cloned.1.call-start = ((), (), s32[]{:S(2)}) async-start(), calls=%async_computation.19 | async-start | bytes 3244032 | tf_op jit(solution)/shard_map/reduce_scatter | solution.py:371
  961.8 628.6 %reduce-scatter.27.cloned.1.call-start = ((), (), s32[]{:S(2)}) async-start(), calls=%async_computation.18 | async-start | bytes 3244032 | tf_op jit(solution)/shard_map/reduce_scatter | solution.py:370
  967.5 698.8 %reduce-scatter.25.cloned.1.call-start = ((), (), s32[]{:S(2)}) async-start(), calls=%async_computation.17 | async-start | bytes 3244032 | tf_op jit(solution)/shard_map/reduce_scatter | solution.py:369
  1090.5 42.4 %copy-start.116 = (f32[1024]{0:T(1024)S(1)}, f32[1024]{0:T(1024)}, u32[]{:S(2)}) copy-start(f32[1024]{0:T(1024)} %copy-done.115) | copy-start | bytes 12292
  1132.9 533.4 %copy-start.1 = (bf16[704,1024]{1,0:T(8,128)(2,1)S(1)}, bf16[704,1024]{1,0:T(8,128)(2,1)}, u32[]{:S(2)}) copy-start(bf16[704,1024]{1,0:T(8,128)(2,1)} %param.50) | copy-start | bytes 4325380
  (123 other events, 327.5 us)
Sparse Core Ops, SparseCore 0:
  474.7 51.6 all-reduce.21
  544.0 51.4 all-reduce.23
  876.1 62.1 reduce-scatter.32
  941.9 60.9 reduce-scatter.30
  1005.8 84.6 all-reduce.25
  1094.7 63.6 reduce-scatter.14
  1162.4 62.3 reduce-scatter.16
  1229.2 67.2 reduce-scatter.22
  1301.1 66.5 reduce-scatter.20
  1372.1 66.5 reduce-scatter.18
  1443.3 71.2 reduce-scatter.28
  1518.9 71.3 reduce-scatter.26
  1594.9 71.3 reduce-scatter.24
where the time goes:
time: 1680 us; the launch traced here: 1670 us
  waiting for transfers between devices  727 us (43%)
  matrix products  427 us (25%)
  other arithmetic  255 us (15%)
  local copies, waits for them, and re-layouts  171 us (10%)
  blocking collectives  66.8 us (4%)
    dot_general x182, matrix products, high_dot(): return jnp.matmul(left, right, precision=maximal_precision)  317 us
    another operation x5, other arithmetic, span_maps(): lax.linalg.triangular_solve(unit_lower, right_side, left_side=True, lower...  162 us
    psum x1, waiting for transfers between devices, per_device(): lax.psum(ffn_part.astype(jnp.bfloat16), 'tensor').astype(jnp.float32)  86.1 us
    reduce_scatter x1, waiting for transfers between devices, per_device(): lax.psum_scatter(gate_grad_w, ('dp', 'ctx'), scatter_dimension=0, tiled=T...  75.9 us
    reduce_scatter x1, waiting for transfers between devices, per_device(): lax.psum_scatter(down_grad_w, ('dp', 'ctx'), scatter_dimension=1, tiled=T...  75.8 us
    reduce_scatter x1, waiting for transfers between devices, per_device(): lax.psum_scatter(up_grad_w, ('dp', 'ctx'), scatter_dimension=0, tiled=True)  75.8 us
    reduce_scatter x1, waiting for transfers between devices, per_device(): lax.psum_scatter(out_grad_w, ('dp', 'ctx'), scatter_dimension=1, tiled=True)  71.8 us
    reduce_scatter x1, waiting for transfers between devices, per_device(): lax.psum_scatter(mixer_w[3], ('dp', 'ctx'), scatter_dimension=0, tiled=True)  71.2 us
  transfers between devices with their start and end apart: 15, of which 13 were waited for; matrix products, arithmetic and copies ran while one was open for 7% of the time, Pallas kernels for 0%

commit v1 on v0

v1 whole, which is shorter than its diff:
```python
import functools

import jax
import jax.numpy as jnp
from jax import lax
from jax.experimental import pallas as pl
from jax.experimental.pallas import tpu as pltpu
from jax.sharding import PartitionSpec as P

KCONV = 4
CHUNK = 128


epsilon = 1e-06
maximal_precision = lax.Precision.HIGHEST


def shifted(value, axis, by):
    devices = lax.axis_size(axis)
    pairs = [(i, i + by) for i in range(devices) if 0 <= i + by < devices]
    return lax.ppermute(value, axis, pairs)


def entering(value, axis, combine, identity, reverse):
    devices, index = (lax.axis_size(axis), lax.axis_index(axis))
    everything = jax.tree.map(
        lambda part, kind: lax.all_gather(part.astype(kind), axis),
        value,
        (jnp.bfloat16, jnp.bfloat16),
    )
    start = jax.tree.map(
        lambda part, zero: jnp.broadcast_to(jnp.asarray(zero, part.dtype), part.shape),
        value,
        identity,
    )

    def lap(k, before):
        at = devices - 1 - k if reverse else k
        reached = at > index if reverse else at < index
        new = combine(
            before, jax.tree.map(lambda part, own: part[at].astype(own.dtype), everything, value)
        )
        return jax.tree.map(lambda a, b: jnp.where(reached, a, b), new, before)

    return lax.fori_loop(0, devices, lap, start)


def high_dot(left, right):
    return jnp.matmul(left, right, precision=maximal_precision)


def flipped(matrix):
    return jnp.swapaxes(matrix, -1, -2)


def span_first(array_in):
    return jnp.moveaxis(array_in, 1, 0)


def rms_gain(rows_in, gain_in):
    return rows_in * lax.rsqrt(jnp.mean(rows_in * rows_in, -1, keepdims=True) + epsilon) * gain_in


def gated_out(head_vals, gate_vals, gain_in):
    return rms_gain(head_vals, gain_in) * jax.nn.silu(gate_vals)


def swiglu(gate_in, up_in):
    return jax.nn.silu(gate_in) * up_in


def dims_dot(left, right, left_dim, right_dim):
    return lax.dot_general(
        left.astype(jnp.bfloat16),
        right.astype(jnp.bfloat16),
        (((left_dim,), (right_dim,)), ((), ())),
        preferred_element_type=jnp.float32,
    )


@jax.custom_vjp
def dot_nn(left, right):
    return dims_dot(left, right, 1, 0)


@jax.custom_vjp
def dot_nt(left, right):
    return dims_dot(left, right, 1, 1)


@jax.custom_vjp
def dot_tn(left, right):
    return dims_dot(left, right, 0, 0)


dot_nn.defvjp(
    lambda l, r: (dims_dot(l, r, 1, 0), (l, r)),
    lambda k, g: (dims_dot(g, k[1], 1, 1), dims_dot(k[0], g, 0, 0)),
)
dot_nt.defvjp(
    lambda l, r: (dims_dot(l, r, 1, 1), (l, r)),
    lambda k, g: (dims_dot(g, k[1], 1, 0), dims_dot(g, k[0], 0, 0)),
)
dot_tn.defvjp(
    lambda l, r: (dims_dot(l, r, 0, 0), (l, r)),
    lambda k, g: (dims_dot(k[1], g, 1, 1), dims_dot(k[0], g, 1, 0)),
)


@jax.custom_vjp
def solve_with(lower, inverse, right):
    return dims_dot(inverse, right, 1, 0)


def solve_fwd(lower, inverse, right):
    found = dims_dot(inverse, right, 1, 0)
    return found, (inverse, found)


def solve_bwd(kept, grad):
    inverse, found = kept
    right_grad = dims_dot(inverse, grad, 0, 0)
    return -dims_dot(right_grad, found, 1, 1), jnp.zeros_like(inverse), right_grad


solve_with.defvjp(solve_fwd, solve_bwd)


def two_parts(value):
    high = value.astype(jnp.bfloat16)
    return high, (value - high.astype(jnp.float32)).astype(jnp.bfloat16)


def grid_indices():
    shape = (CHUNK, CHUNK)
    return lax.broadcasted_iota(jnp.int32, shape, 0), lax.broadcasted_iota(jnp.int32, shape, 1)


def triangle(flip):
    row, col = grid_indices()
    keep = row <= col if flip else row >= col
    return jnp.where(keep, 1.0, 0.0).astype(jnp.bfloat16)


def tri_dot(value, flip):
    tri = triangle(flip)
    high, rest = two_parts(value)
    return dims_dot(tri, high, 1, 0) + dims_dot(tri, rest, 1, 0)


@jax.custom_vjp
def running(value):
    return tri_dot(value, False)


running.defvjp(lambda v: (tri_dot(v, False), None), lambda k, g: (tri_dot(g, True),))


def dot_three(left, right):
    left_high, left_rest = two_parts(left)
    right_high, right_rest = two_parts(right)
    return (
        dims_dot(left_high, right_high, 1, 0)
        + dims_dot(left_high, right_rest, 1, 0)
        + dims_dot(left_rest, right_high, 1, 0)
    )


def unit_inverse(lowers):
    row, col = grid_indices()
    eye = jnp.where(row == col, 1.0, 0.0)
    found = None
    size = 1
    while size < CHUNK:
        pair = (
            (row // (2 * size) == col // (2 * size))
            & (row % (2 * size) >= size)
            & (col % (2 * size) < size)
        )
        corners = [jnp.where(pair, lower, 0.0) for lower in lowers]
        if found is None:
            found = [eye - corner for corner in corners]
        else:
            inner = [dot_three(x, c) for x, c in zip(found, corners)]
            found = [x - dot_three(i, x) for x, i in zip(found, inner)]
        size *= 2
    return found


def decay_parts(gate):
    row, col = grid_indices()
    total = running(gate * jnp.ones((CHUNK, CHUNK), jnp.float32))
    causal = row >= col
    ratio = total - total.T
    decays = jnp.where(causal, jnp.exp(jnp.where(causal, ratio, 0.0)), 0.0)
    last = jnp.sum(jnp.where(row == CHUNK - 1, total, 0.0), 0, keepdims=True)
    tails = jnp.exp(last - total)
    whole = jnp.exp(jnp.sum(gate, 0, keepdims=True))
    return decays, jnp.exp(total), tails, whole


def lower_of(decays, keys, strength):
    row, col = grid_indices()
    return jnp.where(row > col, decays * dot_nt(keys, keys), 0.0) * strength


def chunk_out(queries, keys, values, gate, strength, inverse, state):
    decays, gammas, tails, whole = decay_parts(gate)
    lower = lower_of(decays, keys, strength)
    right = strength * (values - dot_nn(gammas * keys, state))
    fresh = solve_with(lower, inverse, right)
    out = dot_nn(gammas * queries, state) + dot_nn(decays * dot_nt(queries, keys), fresh)
    return out, whole * state + dot_tn(tails * keys, fresh)


def forward_kernel(
    heads, dk, dv, steps,
    q_ref, k_ref, v_ref, gb_ref,
    em_ref, ep_ref, out_ref, inv_ref, mt_ref, s_ref, p_ref, dmap_ref, dadd_ref,
    state, prod,
):
    step = pl.program_id(1)

    @pl.when(step == 0)
    def _():
        row, col = grid_indices()
        state[...] = jnp.zeros_like(state)
        for h in range(heads):
            prod[h] = jnp.where(row == col, 1.0, 0.0)

    parts, lowers = [], []
    for h in range(heads):
        q = q_ref[0, :, h * dk : (h + 1) * dk].astype(jnp.float32)
        k = k_ref[0, :, h * dk : (h + 1) * dk].astype(jnp.float32)
        v = v_ref[0, :, h * dv : (h + 1) * dv].astype(jnp.float32)
        gate = gb_ref[0, h, :, 0:1]
        strength = gb_ref[0, h, :, 1:2]
        decays, gammas, tails, whole = decay_parts(gate)
        lowers.append(lower_of(decays, k, strength))
        parts.append((q, k, v, strength, decays, gammas, tails, whole))
    inverses = unit_inverse(lowers)
    for h in range(heads):
        q, k, v, strength, decays, gammas, tails, whole = parts[h]
        inverse = inverses[h].astype(jnp.bfloat16)
        key_solve = dot_nn(inverse, strength * gammas * k)
        value_solve = dot_nn(inverse, strength * v)
        mixing = decays * dot_nt(q, k)
        emitted = (gammas * q - dot_nn(mixing, key_solve)).astype(jnp.bfloat16)
        tail_keys = tails * k
        minus = dot_tn(tail_keys, key_solve).astype(jnp.bfloat16)
        now_s, now_p = state[h], prod[h]
        inv_ref[0, 0, h] = inverse
        mt_ref[0, 0, h] = minus
        s_ref[0, 0, h] = now_s.astype(jnp.bfloat16)
        p_ref[0, 0, h] = now_p.astype(jnp.bfloat16)
        em_ref[0, :, h * dk : (h + 1) * dk] = emitted
        ep_ref[0, :, h * dk : (h + 1) * dk] = dot_nn(emitted, now_p).astype(jnp.bfloat16)
        out_ref[0, :, h * dv : (h + 1) * dv] = dot_nn(mixing, value_solve) + dot_nn(emitted, now_s)
        new_s = whole * now_s - dot_nn(minus, now_s) + dot_tn(tail_keys, value_solve)
        new_p = whole * now_p - dot_nn(minus, now_p)
        state[h] = new_s
        prod[h] = new_p

        @pl.when(step == steps - 1)
        def _():
            dmap_ref[0, h] = new_p
            dadd_ref[0, h] = new_s


def pull_kernel(
    heads, dk, dv, steps,
    em_ref, mt_ref, gb_ref, grad_ref,
    g_ref, r_ref, pull_ref,
    total, prod,
):
    step = pl.program_id(1)

    @pl.when(step == 0)
    def _():
        row, col = grid_indices()
        total[...] = jnp.zeros_like(total)
        for h in range(heads):
            prod[h] = jnp.where(row == col, 1.0, 0.0)

    for h in range(heads):
        whole = jnp.exp(jnp.sum(gb_ref[0, h, :, 0:1], 0, keepdims=True))
        now_g, now_r = total[h], prod[h]
        g_ref[0, 0, h] = now_g.astype(jnp.bfloat16)
        r_ref[0, 0, h] = now_r.astype(jnp.bfloat16)
        minus = mt_ref[0, 0, h]
        new_g = (
            whole * now_g
            - dot_tn(minus, now_g)
            + dot_tn(em_ref[0, :, h * dk : (h + 1) * dk], grad_ref[0, :, h * dv : (h + 1) * dv])
        )
        total[h] = new_g
        prod[h] = whole * now_r - dot_tn(minus, now_r)

        @pl.when(step == steps - 1)
        def _():
            pull_ref[0, h] = new_g


def backward_kernel(
    heads, dk, dv,
    q_ref, k_ref, v_ref, gb_ref, inv_ref, s_ref, p_ref, in_ref, grad_ref, g_ref, r_ref, suf_ref,
    dq_ref, dk_ref, dv_ref, dgb_ref,
):
    lane = lax.broadcasted_iota(jnp.int32, (CHUNK, CHUNK), 1)
    for h in range(heads):
        q = q_ref[0, :, h * dk : (h + 1) * dk].astype(jnp.float32)
        k = k_ref[0, :, h * dk : (h + 1) * dk].astype(jnp.float32)
        v = v_ref[0, :, h * dv : (h + 1) * dv].astype(jnp.float32)
        gate = gb_ref[0, h, :, 0:1]
        strength = gb_ref[0, h, :, 1:2]
        state = s_ref[0, 0, h].astype(jnp.float32) + dot_nn(p_ref[0, 0, h], in_ref[0, h])
        after = g_ref[0, 0, h].astype(jnp.float32) + dot_nn(r_ref[0, 0, h], suf_ref[0, h])
        inverse = inv_ref[0, 0, h]
        unused, back = jax.vjp(
            lambda *five: chunk_out(*five, inverse, state), q, k, v, gate, strength
        )
        dq, dkk, dvv, dgate, dstrength = back((grad_ref[0, :, h * dv : (h + 1) * dv], after))
        dq_ref[0, :, h * dk : (h + 1) * dk] = dq
        dk_ref[0, :, h * dk : (h + 1) * dk] = dkk
        dv_ref[0, :, h * dv : (h + 1) * dv] = dvv
        dgb_ref[0, h] = jnp.where(lane == 0, dgate, jnp.where(lane == 1, dstrength, 0.0))


def kernel_specs(heads, dk, dv, steps, reverse):
    def at(c):
        return steps - 1 - c if reverse else c

    return {
        "k": pl.BlockSpec((1, CHUNK, heads * dk), lambda s, c: (s, at(c), 0)),
        "v": pl.BlockSpec((1, CHUNK, heads * dv), lambda s, c: (s, at(c), 0)),
        "gb": pl.BlockSpec((1, heads, CHUNK, CHUNK), lambda s, c: (s, 0, at(c), 0)),
        "kk": pl.BlockSpec((1, 1, heads, dk, dk), lambda s, c: (s, at(c), 0, 0, 0)),
        "kv": pl.BlockSpec((1, 1, heads, dk, dv), lambda s, c: (s, at(c), 0, 0, 0)),
        "dkk": pl.BlockSpec((1, heads, dk, dk), lambda s, c: (s, 0, 0, 0)),
        "dkv": pl.BlockSpec((1, heads, dk, dv), lambda s, c: (s, 0, 0, 0)),
    }


def kernel_call(body, grid, ins, outs, scratch=()):
    return pl.pallas_call(
        body,
        grid=grid,
        in_specs=ins,
        out_specs=[o[0] for o in outs],
        out_shape=[jax.ShapeDtypeStruct(o[1], o[2]) for o in outs],
        scratch_shapes=list(scratch),
        compiler_params=pltpu.CompilerParams(
            dimension_semantics=("arbitrary", "arbitrary"), vmem_limit_bytes=40 * 1024 * 1024
        ),
    )


def combine_maps(earlier, later):
    return (high_dot(later[0], earlier[0]), high_dot(later[0], earlier[1]) + later[1])


def identity_maps(carry_map, carry_add):
    lane_count = carry_map.shape[0]
    key_dim = carry_map.shape[-1]
    eye_block = jnp.broadcast_to(
        jnp.eye(key_dim, dtype=jnp.float32), (lane_count, key_dim, key_dim)
    )
    return (eye_block, jnp.zeros((lane_count,) + carry_add.shape[-2:], jnp.float32))


def rows_dot(left, right):
    return lax.dot_general(
        left, right, (((0,), (0,)), ((), ())), preferred_element_type=jnp.float32
    ).astype(jnp.bfloat16)


def summed_over_rows(partial):
    return lax.psum_scatter(
        partial, ("dp", "ctx"), scatter_dimension=0, tiled=True
    ).astype(jnp.float32)


def scattered(left, right):
    return summed_over_rows(rows_dot(left, right))


def per_device(
    tokens,
    first_gain,
    query_weight,
    key_weight,
    value_weight,
    outgate_weight,
    alpha_weight,
    beta_weight,
    query_conv,
    convolved_keys,
    value_conv,
    decay_rate,
    time_bias,
    head_gain,
    out_weight,
    second_gain,
    gate_weight,
    up_weight,
    down_weight,
    cotangent,
):
    seq_count, local_len, model_width = tokens.shape
    rows = seq_count * local_len
    heads = decay_rate.shape[0]
    q_cols = query_weight.shape[1]
    k_cols = key_weight.shape[1]
    v_cols = value_weight.shape[1]
    key_dim = q_cols // heads
    val_dim = v_cols // heads
    steps = local_len // CHUNK
    lane_count = seq_count * heads

    def mixer_front(padded_in, kernel_in, alpha_in, beta_in, decay_in, bias_in):
        summed = sum(
            (
                kernel_in[tap_index] * padded_in[:, tap_index : tap_index + local_len, :]
                for tap_index in range(KCONV)
            )
        )
        active = jax.nn.silu(summed)
        def unit(first, width):
            pieces = [active[..., first + h * width : first + (h + 1) * width] for h in range(heads)]
            return jnp.concatenate(
                [p * lax.rsqrt(jnp.sum(p * p, -1, keepdims=True) + epsilon) for p in pieces], -1
            )

        unit_query = unit(0, key_dim) * key_dim ** (-0.5)
        unit_key = unit(q_cols, key_dim)
        raw_value = active[..., q_cols + k_cols :]
        log_gate = -decay_in * jax.nn.softplus(
            alpha_in.reshape(seq_count, local_len, heads) + bias_in
        )
        strength = jax.nn.sigmoid(beta_in.reshape(seq_count, local_len, heads))
        both = jnp.stack([log_gate, strength], -1)
        both = jnp.transpose(both, (0, 2, 1, 3))
        both = jnp.pad(both, ((0, 0), (0, 0), (0, 0), (0, CHUNK - 2)))
        return (unit_query, unit_key, raw_value, both)

    inputs = tokens.reshape(rows, model_width).astype(jnp.float32)
    normed1, norm1_back = jax.vjp(rms_gain, inputs, first_gain)
    normed1_b = normed1.astype(jnp.bfloat16)

    def project(weight):
        return jnp.dot(normed1_b, weight, preferred_element_type=jnp.float32)

    linear = jnp.concatenate([project(query_weight), project(key_weight), project(value_weight)], 1)
    linear = linear.astype(jnp.bfloat16).reshape(seq_count, local_len, q_cols + k_cols + v_cols)
    gate_lin = project(outgate_weight)
    alpha_lin = project(alpha_weight)
    beta_lin = project(beta_weight)
    rims = shifted(linear[:, local_len - (KCONV - 1) :, :], "ctx", 1)
    padded = jnp.concatenate([rims, linear], 1).astype(jnp.float32)
    kernel = jnp.concatenate([query_conv, convolved_keys, value_conv], 1)
    front_out, front_back = jax.vjp(
        mixer_front, padded, kernel, alpha_lin, beta_lin, decay_rate, time_bias
    )
    queries = front_out[0].astype(jnp.bfloat16)
    keys_in = front_out[1].astype(jnp.bfloat16)
    values_in = front_out[2].astype(jnp.bfloat16)
    both = front_out[3]
    grid = (seq_count, steps)
    low, full = jnp.bfloat16, jnp.float32
    k_rows, v_rows = (seq_count, local_len, q_cols), (seq_count, local_len, v_cols)
    kk = (seq_count, steps, heads, key_dim, key_dim)
    kv = (seq_count, steps, heads, key_dim, val_dim)
    dkk, dkv = (seq_count,) + kk[2:], (seq_count,) + kv[2:]
    spec = kernel_specs(heads, key_dim, val_dim, steps, False)
    carries = (
        pltpu.VMEM((heads, key_dim, val_dim), full),
        pltpu.VMEM((heads, key_dim, key_dim), full),
    )
    emitted, emitted_in, head_local, inverse, minus, states, prods, device_map, device_add = kernel_call(
        functools.partial(forward_kernel, heads, key_dim, val_dim, steps),
        grid,
        [spec["k"], spec["k"], spec["v"], spec["gb"]],
        [
            (spec["k"], k_rows, low),
            (spec["k"], k_rows, low),
            (spec["v"], v_rows, full),
            (spec["kk"], kk, low),
            (spec["kk"], kk, low),
            (spec["kv"], kv, low),
            (spec["kk"], kk, low),
            (spec["dkk"], dkk, full),
            (spec["dkv"], dkv, full),
        ],
        carries,
    )(queries, keys_in, values_in, both)
    device_map = device_map.reshape(lane_count, key_dim, key_dim)
    device_add = device_add.reshape(lane_count, key_dim, val_dim)
    prefix = entering(
        (device_map, device_add), "ctx", combine_maps, identity_maps(device_map, device_add), False
    )
    state_in = prefix[1].astype(low).reshape(dkv)
    head_out = jnp.stack(
        [
            head_local[..., h * val_dim : (h + 1) * val_dim]
            + jnp.einsum(
                "stk,skv->stv",
                emitted_in[..., h * key_dim : (h + 1) * key_dim],
                state_in[:, h],
                preferred_element_type=full,
            )
            for h in range(heads)
        ],
        2,
    )
    gate_heads = gate_lin.reshape(seq_count, local_len, heads, val_dim)
    normed_heads, gated_back = jax.vjp(gated_out, head_out, gate_heads, head_gain)
    normed_heads_b = normed_heads.reshape(rows, v_cols).astype(jnp.bfloat16)
    mixer_part = jnp.dot(normed_heads_b, out_weight, preferred_element_type=jnp.float32)
    middle = inputs + lax.psum(mixer_part.astype(jnp.bfloat16), "tensor").astype(jnp.float32)
    normed2, second_norm_backward = jax.vjp(rms_gain, middle, second_gain)
    normed2_b = normed2.astype(jnp.bfloat16)
    gate_pre = jnp.dot(normed2_b, gate_weight, preferred_element_type=jnp.float32)
    up_pre = jnp.dot(normed2_b, up_weight, preferred_element_type=jnp.float32)
    hidden_f, swiglu_back = jax.vjp(swiglu, gate_pre, up_pre)
    hidden = hidden_f.astype(jnp.bfloat16)
    ffn_part = jnp.dot(hidden, down_weight, preferred_element_type=jnp.float32)
    block_out = (
        middle + lax.psum(ffn_part.astype(jnp.bfloat16), "tensor").astype(jnp.float32)
    ).astype(jnp.bfloat16)
    grad_rows = cotangent.reshape(rows, model_width)
    hidden_grad = jnp.dot(grad_rows, down_weight.T, preferred_element_type=jnp.float32)
    gate_grad, up_grad = swiglu_back(hidden_grad)
    gate_grad_b = gate_grad.astype(jnp.bfloat16)
    up_grad_b = up_grad.astype(jnp.bfloat16)
    normed2_part = jnp.dot(gate_grad_b, gate_weight.T, preferred_element_type=jnp.float32)
    normed2_part = normed2_part + jnp.dot(
        up_grad_b, up_weight.T, preferred_element_type=jnp.float32
    )
    normed2_grad = lax.psum(normed2_part.astype(jnp.bfloat16), "tensor").astype(jnp.float32)
    middle_norm_grad, second_gain_grad = second_norm_backward(normed2_grad)
    middle_grad = grad_rows.astype(jnp.float32) + middle_norm_grad
    middle_low = middle_grad.astype(jnp.bfloat16)
    ffn_cols = gate_weight.shape[1]
    ffn_w = summed_over_rows(
        jnp.concatenate(
            [
                rows_dot(normed2_b, jnp.concatenate([gate_grad_b, up_grad_b], 1)),
                rows_dot(grad_rows, hidden),
            ],
            1,
        )
    )
    out_w = scattered(middle_low, normed_heads_b)
    heads_grad = jnp.dot(middle_low, out_weight.T, preferred_element_type=jnp.float32).reshape(
        seq_count, local_len, heads, val_dim
    )
    head_out_grad, head_gate_gradient, head_gain_grad = gated_back(heads_grad)
    out_grad = head_out_grad.reshape(v_rows)
    back_spec = kernel_specs(heads, key_dim, val_dim, steps, True)
    pulls, suffixes, local_pull = kernel_call(
        functools.partial(pull_kernel, heads, key_dim, val_dim, steps),
        grid,
        [back_spec["k"], back_spec["kk"], back_spec["gb"], back_spec["v"]],
        [
            (back_spec["kv"], kv, low),
            (back_spec["kk"], kk, low),
            (back_spec["dkv"], dkv, full),
        ],
        carries,
    )(emitted, minus, both, out_grad)
    suffix = entering(
        (flipped(device_map), local_pull.reshape(lane_count, key_dim, val_dim)),
        "ctx",
        combine_maps,
        identity_maps(device_map, device_add),
        True,
    )
    suffix_in = suffix[1].astype(low).reshape(dkv)
    query_grad, key_grad, value_grad, both_grad = kernel_call(
        functools.partial(backward_kernel, heads, key_dim, val_dim),
        grid,
        [
            spec["k"], spec["k"], spec["v"], spec["gb"], spec["kk"], spec["kv"], spec["kk"],
            spec["dkv"], spec["v"], spec["kv"], spec["kk"], spec["dkv"],
        ],
        [
            (spec["k"], k_rows, full),
            (spec["k"], k_rows, full),
            (spec["v"], v_rows, full),
            (spec["gb"], both.shape, full),
        ],
    )(
        queries, keys_in, values_in, both, inverse, states, prods,
        state_in, out_grad, pulls, suffixes, suffix_in,
    )
    padded_grad, kernel_grad, alpha_grad, beta_grad, decay_grad, bias_grad = front_back(
        (query_grad, key_grad, value_grad, both_grad)
    )
    rim_back = shifted(padded_grad[:, : KCONV - 1, :].astype(jnp.bfloat16), "ctx", -1).astype(
        jnp.float32
    )
    linear_grad = padded_grad[:, KCONV - 1 :, :] + jnp.pad(
        rim_back, ((0, 0), (local_len - (KCONV - 1), 0), (0, 0))
    )
    linear_grad_b = linear_grad.reshape(rows, q_cols + k_cols + v_cols).astype(jnp.bfloat16)
    query_lin_grad = linear_grad_b[:, :q_cols]
    key_lin_grad = linear_grad_b[:, q_cols : q_cols + k_cols]
    value_lin_grad = linear_grad_b[:, q_cols + k_cols :]
    gate_lin_grad = head_gate_gradient.reshape(rows, v_cols).astype(jnp.bfloat16)
    alpha_lin_grad = alpha_grad.astype(jnp.bfloat16)
    beta_lin_grad = beta_grad.astype(jnp.bfloat16)
    paired = (
        (query_weight, query_lin_grad),
        (key_weight, key_lin_grad),
        (value_weight, value_lin_grad),
        (outgate_weight, gate_lin_grad),
        (alpha_weight, alpha_lin_grad),
        (beta_weight, beta_lin_grad),
    )
    normed1_part = sum(
        (jnp.dot(grad_b, weight.T, preferred_element_type=jnp.float32) for weight, grad_b in paired)
    )
    late_cols = jnp.concatenate([linear_grad_b, alpha_lin_grad, beta_lin_grad], 1)
    late_w = scattered(normed1_b, late_cols)
    gate_w = scattered(normed1_b, gate_lin_grad)
    normed1_grad = lax.psum(normed1_part.astype(jnp.bfloat16), "tensor").astype(jnp.float32)
    inputs_norm_grad, first_gain_grad = norm1_back(normed1_grad)
    tokens_grad = (middle_grad + inputs_norm_grad).astype(jnp.bfloat16)
    v_end = q_cols + k_cols + v_cols
    weight_grads = (
        late_w[:, :q_cols],
        late_w[:, q_cols : q_cols + k_cols],
        late_w[:, q_cols + k_cols : v_end],
        gate_w,
        late_w[:, v_end : v_end + heads],
        late_w[:, v_end + heads :],
        out_w.T,
        ffn_w[:, :ffn_cols],
        ffn_w[:, ffn_cols : 2 * ffn_cols],
        ffn_w[:, 2 * ffn_cols :].T,
    )
    index = lax.axis_index("tensor")
    first_own = jnp.where(index == 0, 1.0, 0.0)
    gains = lax.psum(
        jnp.concatenate([first_own * first_gain_grad, first_own * second_gain_grad, head_gain_grad]),
        ("dp", "ctx", "tensor"),
    )
    smalls = lax.psum(
        jnp.concatenate([kernel_grad.reshape(-1), decay_grad, bias_grad]), ("dp", "ctx")
    )
    taps = kernel_grad.size
    small_sums = (
        gains[:model_width],
        gains[model_width : 2 * model_width],
        gains[2 * model_width :],
        smalls[:taps].reshape(kernel_grad.shape),
        smalls[taps : taps + heads],
        smalls[taps + heads :],
    )
    kernel_sum = small_sums[3]
    return (
        block_out.reshape(seq_count, local_len, model_width),
        tokens_grad.reshape(seq_count, local_len, model_width),
        small_sums[0],
        weight_grads[0],
        weight_grads[1],
        weight_grads[2],
        weight_grads[3],
        weight_grads[4],
        weight_grads[5],
        kernel_sum[:, :q_cols],
        kernel_sum[:, q_cols : q_cols + k_cols],
        kernel_sum[:, q_cols + k_cols :],
        small_sums[4],
        small_sums[5],
        small_sums[2],
        weight_grads[6],
        small_sums[1],
        weight_grads[7],
        weight_grads[8],
        weight_grads[9],
    )


def solution(mesh):
    placed = (
        P("dp", "ctx", None),
        P(),
        P(None, "tensor"),
        P(None, "tensor"),
        P(None, "tensor"),
        P(None, "tensor"),
        P(None, "tensor"),
        P(None, "tensor"),
        P(None, "tensor"),
        P(None, "tensor"),
        P(None, "tensor"),
        P("tensor"),
        P("tensor"),
        P(),
        P("tensor", None),
        P(),
        P(None, "tensor"),
        P(None, "tensor"),
        P("tensor", None),
        P("dp", "ctx", None),
    )
    return jax.shard_map(
        per_device,
        mesh=mesh,
        in_specs=placed,
        out_specs=(
            P("dp", "ctx", None),
            P("dp", "ctx", None),
            P(),
            P(("dp", "ctx"), "tensor"),
            P(("dp", "ctx"), "tensor"),
            P(("dp", "ctx"), "tensor"),
            P(("dp", "ctx"), "tensor"),
            P(("dp", "ctx"), "tensor"),
            P(("dp", "ctx"), "tensor"),
            P(None, "tensor"),
            P(None, "tensor"),
            P(None, "tensor"),
            P("tensor"),
            P("tensor"),
            P(),
            P("tensor", ("dp", "ctx")),
            P(),
            P(("dp", "ctx"), "tensor"),
            P(("dp", "ctx"), "tensor"),
            P("tensor", ("dp", "ctx")),
        ),
        check_vma=False,
    )
```

time: 1680 us -> 730 us (0.43)
  waiting for transfers between devices: 727 us -> 274 us
  matrix products: 427 us -> 81.6 us
  other arithmetic: 255 us -> 75.7 us
  local copies, waits for them, and re-layouts: 171 us -> 112 us
  Pallas kernels: 0 us -> 50 us
  blocking collectives: 66.8 us -> 102 us
    reduce_scatter x8 -> x3, waiting for transfers between devices: 526 us -> 90.6 us  [summed_over_rows(): lax.psum_scatter(partial, ('dp', 'ctx'), scatter_dimension=0, tiled=True)]
    dot_general x182 -> x4, matrix products: 317 us -> 4.95 us  [high_dot(): return jnp.matmul(left, right, precision=maximal_precision)]
    another operation x8 -> x2, other arithmetic: 164 us -> 1.15 us  [the longest x5 162 us: span_maps(): lax.linalg.triangular_solve(unit_lower, right_side, left_side=True, lower...]
    while x70 -> x4, local copies, waits for them, and re-layouts: 51.2 us -> 0.07 us
    pallas_call x0 -> x3, Pallas kernels: none -> 50 us  [the longest x1 26.6 us: per_device(): kernel_call(functools.partial(forward_kernel, heads, key_dim, val_dim, st...]
    dynamic_update_slice x48 -> x0, local copies, waits for them, and re-layouts: 48.4 us -> none  [run_spans(): lax.scan(advance, state_in, (span_first(emitted), span_first(offsets), sp...]
    psum x2, blocking collectives: 43.5 us -> 78.8 us  [the longest x1 40.5 us: per_device(): lax.psum(jnp.concatenate([first_own * first_gain_grad, first_own * second...]
    pallas_call x0 -> x1, local copies, waits for them, and re-layouts: none -> 30 us  [per_device(): kernel_call(functools.partial(backward_kernel, heads, key_dim, val_dim),...]
  transfers between devices with their start and end apart: 15 -> 9, of which waited for: 13 -> 5; matrix products, arithmetic and copies ran while one was open for 7% -> 25% of each run, Pallas kernels for 0% -> 3%
where the time goes in v1:
time: 730 us; the launch traced here: 720 us
  waiting for transfers between devices  274 us (38%)
  local copies, waits for them, and re-layouts  112 us (15%)
  blocking collectives  102 us (14%)
  matrix products  81.6 us (11%)
  other arithmetic  75.7 us (10%)
  Pallas kernels  50 us (7%)
  between operations  16.1 us (2%)
  starting transfers between devices  7.67 us (1%)
    reduce_scatter x3, waiting for transfers between devices, summed_over_rows(): lax.psum_scatter(partial, ('dp', 'ctx'), scatter_dimension=0, tiled=True)  90.6 us
    psum x1, waiting for transfers between devices, per_device(): lax.psum(ffn_part.astype(jnp.bfloat16), 'tensor').astype(jnp.float32)  72.6 us
    psum x1, waiting for transfers between devices, per_device(): lax.psum(mixer_part.astype(jnp.bfloat16), 'tensor').astype(jnp.float32)  51.6 us
    psum x1, blocking collectives, per_device(): lax.psum(jnp.concatenate([first_own * first_gain_grad, first_own * second...  40.5 us
    psum x1, waiting for transfers between devices, per_device(): lax.psum(normed2_part.astype(jnp.bfloat16), 'tensor').astype(jnp.float32)  38.5 us
    psum x1, blocking collectives, per_device(): lax.psum(jnp.concatenate([kernel_grad.reshape(-1), decay_grad, bias_grad]...  38.3 us
    unnamed x273, local copies, waits for them, and re-layouts  37.8 us
    pallas_call x1, local copies, waits for them, and re-layouts, per_device(): kernel_call(functools.partial(backward_kernel, heads, key_dim, val_dim),...  30 us
  transfers between devices with their start and end apart: 9, of which 5 were waited for; matrix products, arithmetic and copies ran while one was open for 25% of the time, Pallas kernels for 3%

profile of v1, /device:TPU:0, one launch (start us, length us, event | category | flops | bytes accessed | tf_op | source)
XLA Modules:
  0.0 719.8 jit_solution(8598474414340288016)
XLA Ops:
  15.8 5.4 collective-permute-start
  24.8 7.6 %copy.195 = f32[1,1024,2,1]{3,1,2,0:T(8,128)} copy(f32[1,1024,2,1]{2,1,3,0:T(8,128)S(1)} %multiply_bitcast_fusion) | data formatting | bytes 16384 | tf_op jit(solution)/shard_map/jvp()/stack | solution.py:441
  32.4 3.2 fusion.64
  35.6 8.6 %copy.196 = f32[1,1024,2,1]{3,1,2,0:T(8,128)} copy(f32[1,1024,2,1]{2,1,3,0:T(8,128)} %bitcast.216) | data formatting | bytes 16384 | tf_op jit(solution)/shard_map/jvp()/stack | solution.py:441
  44.3 4.0 fusion.99
  49.6 3.1 copy.202
  56.0 3.9 fusion.32
  62.7 26.6 %shard_map.347 = (bf16[1,1024,256]{2,1,0:T(8,128)(2,1)S(1)}, bf16[1,1024,256]{2,1,0:T(8,128)(2,1)S(1)}, f32[1,1024,512]{2,1,0:T(8,128)S(1)}, bf16[1,8,2,128,128]...) custom-call(bf16[1,1024,256]{2,1,0:T(8,128)(2,1)S(1)} %fusion.66.q_r, ...), custom_call_target="tpu_custom_call" | custom-call | tf_op jit(solution)/shard_map/pallas_call | solution.py:479
  91.7 5.8 all_gather.19
  97.5 4.9 all_gather.18
  121.0 51.6 %all-reduce.20.cloned.1.call-done = bf16[1024,1024]{1,0:T(8,128)(2,1)} async-done(((bf16[1024,1024]{1,0:T(8,128)(2,1)}), bf16[1024,1024]{1,0:T(8,128)(2,1)}) %all-reduce.20.cloned.1.call-update) | async-done | bytes 2097168 | tf_op jit(solution)/shard_map/psum | solution.py:519
  172.6 3.1 multiply_reduce_fusion.4
  181.3 3.9 multiply_convert_fusion.1
  187.0 3.3 add_convert_fusion.1
  190.4 3.0 copy.205
  193.5 5.5 all-gather
  199.0 4.5 convolution_convert_fusion.3
  203.5 38.5 %all-reduce.22.cloned.1.call-done = bf16[1024,1024]{1,0:T(8,128)(2,1)} async-done(((bf16[1024,1024]{1,0:T(8,128)(2,1)}), bf16[1024,1024]{1,0:T(8,128)(2,1)}) %all-reduce.22.cloned.1.call-update) | async-done | bytes 2097168 | tf_op jit(solution)/shard_map/psum | solution.py:539
  242.0 5.4 fusion.22
  248.0 5.3 convolution_convert_fusion.4
  253.4 6.6 fusion.68
  260.0 2.9 copy.203
  262.9 3.0 copy.206
  266.0 3.0 multiply_reduce_fusion.6
  272.2 4.3 multiply_reduce_fusion.5
  276.5 4.0 shard_map.348
  282.3 7.2 all_gather.22
  301.0 19.4 %shard_map.349 = (f32[1,1024,256]{2,1,0:T(8,128)S(1)}, f32[1,1024,256]{2,1,0:T(8,128)S(1)}, f32[1,1024,512]{2,1,0:T(8,128)S(1)}, f32[1,2,1024,128]{3,2,1,0:T(8,128)S(1)}) custom-call(bf16[1,1024,256]{2,1,0:T(8,128)(2,1)S(1)} %copy-done.5, bf16[1,1024,256]{2,1,0:T(8,128)(2,1)S(1)} %copy-done.7, bf16[1,1024,512]{2,1,0:T(8,128)(2,1)S(1)} %copy-done.3, ...), custom_call_target="tpu_custom_call" | custom-call | tf_op jit(solution)/shard_map/pallas_call | solution.py:579
  323.8 3.4 multiply_reduce_fusion.3
  327.3 6.0 broadcast_multiply_fusion
  333.3 8.9 %pad_add_fusion = f32[1,1027,1024]{2,1,0:T(8,128)} fusion(f32[1,1024,1024]{2,1,0:T(8,128)} %get-tuple-element.511, f32[1,1024,1024]{2,1,0:T(8,128)} %get-tuple-element.512, f32[1,1024,1024]{2,1,0:T(8,128)} %get-tuple-element.513, f32[1,1024,1024]{2,1,0:T(8,128)S(1)} %get-tuple-element.510), kind=kLoop, calls=%fused_computation.36 | loop fusion | flops 3154944 | bytes 20983808 | tf_op jit(solution)/shard_map/transpose(jvp())/add_any | solution.py:423
  342.2 30.0 %copy.211 = f32[1,2,1024,128]{1,2,3,0:T(8,128)} copy(f32[1,2,1024,128]{3,2,1,0:T(8,128)S(1)} %copy-done.11) | data formatting | bytes 2097152 | tf_op jit(solution)/shard_map/pallas_call | solution.py:579
  376.5 2.7 fusion.104
  381.4 3.3 fusion.103
  384.7 2.8 fusion.105
  387.6 2.8 fusion.45
  394.5 5.8 add_convert_fusion
  400.4 3.1 concatenate.114
  403.5 4.7 convolution_convert_fusion
  411.1 3.7 fusion.55
  415.5 5.9 convolution_convert_fusion.1
  424.1 38.3 %psum.47 = f32[4100]{0:T(1024)S(1)} all-reduce(f32[4100]{0:T(1024)S(1)} %concatenate.115), channel_id=1, replica_groups=mesh['dp'=4,'ctx'=2,'tensor'=4] {'dp','ctx'}, use_global_device_ids=true, to_apply=%region_35.36 | all-reduce | flops 4100 | bytes 32800 | tf_op jit(solution)/shard_map/psum | solution.py:648
  467.6 72.6 %all-reduce.24.cloned.1.call-done = (bf16[1024,1024]{1,0:T(8,128)(2,1)}, bf16[1024,1024]{1,0:T(8,128)(2,1)}) async-done(((bf16[1024,1024]{1,0:T(8,128)(2,1)}, bf16[1024,1024]{1,0:T(8,128)(2,1)}), (bf16[1024,1024]{1,0:T(8,128)(2,1)}, bf16[1024,1024]{1,0:T(8,128)(2,1)})) %all-reduce.24.cloned.1.call-update) | async-done | bytes 4194320 | tf_op jit(solution)/shard_map/psum | solution.py:528
  540.2 3.3 fusion.23
  543.5 40.5 %psum.46 = f32[2304]{0:T(1024)S(1)} all-reduce(f32[2304]{0:T(1024)S(1)} %pad_maximum_fusion.3), channel_id=1, replica_groups=mesh['dp'=4,'ctx'=2,'tensor'=4] {'dp','ctx','tensor'}, use_global_device_ids=true, to_apply=%region_26.27 | all-reduce | flops 2304 | bytes 18432 | tf_op jit(solution)/shard_map/psum | solution.py:644
  585.3 7.4 %fusion.46 = (bf16[1,1024,1024]{2,1,0:T(8,128)(2,1)}, bf16[1,1024,1024]{2,1,0:T(8,128)(2,1)}) fusion(bf16[1024,1024]{1,0:T(8,128)(2,1)} %get-tuple-element.490, bf16[1,1024,1024]{2,1,0:T(8,128)(2,1)S(1)} %copy-done.32, f32[1024]{0:T(1024)S(1)} %multiply_multiply_fusion.1, f32[1024]{0:T(1024)S(1)} %copy-done.95, f32[1024]{0:T(1024)S(1)} %copy-done.73, ...), kind=kLoop, calls=%fused_computation.83 | loop fusion | flops 23068672 | bytes 16801792 | tf_op jit(solution)/shard_map/reshape | solution.py:663
  592.7 21.0 %reduce-scatter.13.cloned.1.call-done = bf16[128,1028]{1,0:T(8,128)(2,1)} async-done(((bf16[1024,1028]{1,0:T(8,128)(2,1)}), bf16[128,1028]{1,0:T(8,128)(2,1)}) %reduce-scatter.13.cloned.1.call-update) | async-done | bytes 263184
  617.7 90.6 %reduce-scatter.11.cloned.1.call-done = bf16[128,2112]{1,0:T(8,128)(2,1)} async-done(((bf16[1024,2112]{1,0:T(8,128)(2,1)}), bf16[128,2112]{1,0:T(8,128)(2,1)}) %reduce-scatter.11.cloned.1.call-update) | async-done | bytes 540688 | tf_op jit(solution)/shard_map/reduce_scatter | solution.py:378
  (392 shorter events, 104.2 us)
Async XLA Ops:
  7.2 174.1 %copy-start = (bf16[704,1024]{1,0:T(8,128)(2,1)S(1)}, bf16[704,1024]{1,0:T(8,128)(2,1)}, u32[]{:S(2)}) copy-start(bf16[704,1024]{1,0:T(8,128)(2,1)} %param.42) | copy-start | bytes 4325380
  7.2 165.4 %all-reduce.20.cloned.1.call-start = ((), (), s32[]{:S(2)}) async-start(), calls=%async_computation.4 | async-start | bytes 4194304 | tf_op jit(solution)/shard_map/psum | solution.py:519
  7.3 4.7 copy-start.64
  11.9 11.0 %copy-start.51 = (bf16[1024,1024]{1,0:T(8,128)(2,1)}, bf16[1024,1024]{1,0:T(8,128)(2,1)S(1)}, u32[]{:S(2)}) copy-start(bf16[1024,1024]{1,0:T(8,128)(2,1)S(1)} %fusion.20) | copy-start | bytes 6291460
  15.1 7.7 %copy-start.113 = (f32[4,256]{1,0:T(4,128)S(1)}, f32[4,256]{1,0:T(4,128)}, u32[]{:S(2)}) copy-start(f32[4,256]{1,0:T(4,128)} %param.32) | copy-start | bytes 12292
  15.1 7.7 %copy-start.114 = (f32[4,256]{1,0:T(4,128)S(1)}, f32[4,256]{1,0:T(4,128)}, u32[]{:S(2)}) copy-start(f32[4,256]{1,0:T(4,128)} %param.33) | copy-start | bytes 12292
  15.2 7.7 %copy-start.111 = (f32[4,512]{1,0:T(4,128)S(1)}, f32[4,512]{1,0:T(4,128)}, u32[]{:S(2)}) copy-start(f32[4,512]{1,0:T(4,128)} %param.34) | copy-start | bytes 24580
  15.2 7.7 %copy-start.123 = (f32[2]{0:T(128)S(1)}, f32[2]{0:T(128)}, u32[]{:S(2)}) copy-start(f32[2]{0:T(128)} %param.35) | copy-start | bytes 28
  15.2 7.8 %copy-start.106 = (bf16[1024,2]{0,1:T(2,128)(2,1)S(1)}, bf16[1024,2]{0,1:T(2,128)(2,1)}, u32[]{:S(2)}) copy-start(bf16[1024,2]{0,1:T(2,128)(2,1)} %param.30) | copy-start | bytes 12292
  15.2 7.8 %copy-start.118 = (f32[2]{0:T(128)S(1)}, f32[2]{0:T(128)}, u32[]{:S(2)}) copy-start(f32[2]{0:T(128)} %param.36) | copy-start | bytes 28
  15.8 38.8 %collective-permute-start = (bf16[1,3,1024]{2,1,0:T(4,128)(2,1)}, bf16[1,3,1024]{2,1,0:T(4,128)(2,1)}, u32[]{:S(2)}, u32[]{:S(2)}) collective-permute-start(bf16[1,3,1024]{2,1,0:T(4,128)(2,1)} %pad_maximum_fusion.4), channel_id=1, source_target_pairs={{0,4},{1,5},{2,6},{3,7},{8,12},{9,13},{10,14},{11,15},{16,20},{17,... | collective-permute-start | bytes 18440 | tf_op jit(solution)/shard_map/ppermute | solution.py:21
  22.9 33.0 %copy-start.96 = (f32[1,1024]{1,0:T(1,128)}, f32[1,1024]{1,0:T(1,128)S(1)}, u32[]{:S(2)}) copy-start(f32[1,1024]{1,0:T(1,128)S(1)} %get-tuple-element.534) | copy-start | bytes 12292
  22.9 33.0 %copy-start.98 = (f32[1,1024]{1,0:T(1,128)}, f32[1,1024]{1,0:T(1,128)S(1)}, u32[]{:S(2)}) copy-start(f32[1,1024]{1,0:T(1,128)S(1)} %get-tuple-element.535) | copy-start | bytes 12292
  22.9 33.0 %copy-start.100 = (f32[1,1024]{1,0:T(1,128)}, f32[1,1024]{1,0:T(1,128)S(1)}, u32[]{:S(2)}) copy-start(f32[1,1024]{1,0:T(1,128)S(1)} %get-tuple-element.536) | copy-start | bytes 12292
  22.9 33.0 %copy-start.102 = (f32[1,1024]{1,0:T(1,128)}, f32[1,1024]{1,0:T(1,128)S(1)}, u32[]{:S(2)}) copy-start(f32[1,1024]{1,0:T(1,128)S(1)} %get-tuple-element.537) | copy-start | bytes 12292
  32.4 11.9 %copy-start.52 = (bf16[1024,1024]{1,0:T(8,128)(2,1)S(1)}, bf16[1024,1024]{1,0:T(8,128)(2,1)}, u32[]{:S(2)}) copy-start(bf16[1024,1024]{1,0:T(8,128)(2,1)} %copy-done.51) | copy-start | bytes 6291460
  62.5 39.9 %copy-start.6 = (bf16[1,1024,256]{2,1,0:T(8,128)(2,1)}, bf16[1,1024,256]{2,1,0:T(8,128)(2,1)S(1)}, u32[]{:S(2)}) copy-start(bf16[1,1024,256]{2,1,0:T(8,128)(2,1)S(1)} %pad_maximum_fusion.2.k_ref) | copy-start | bytes 1572868
  62.7 26.6 %copy-start.4 = (bf16[1,1024,256]{2,1,0:T(8,128)(2,1)}, bf16[1,1024,256]{2,1,0:T(8,128)(2,1)S(1)}, u32[]{:S(2)}) copy-start(bf16[1,1024,256]{2,1,0:T(8,128)(2,1)S(1)} %fusion.66.q_ref) | copy-start | bytes 1572868
  91.7 10.7 %copy-start.8 = (f32[1,1024,512]{2,1,0:T(8,128)}, f32[1,1024,512]{2,1,0:T(8,128)S(1)}, u32[]{:S(2)}) copy-start(f32[1,1024,512]{2,1,0:T(8,128)S(1)} %get-tuple-element.262) | copy-start | bytes 6291460
  91.7 10.8 %copy-start.12 = (bf16[1,8,2,128,256]{4,3,2,1,0:T(8,128)(2,1)}, bf16[1,8,2,128,256]{4,3,2,1,0:T(8,128)(2,1)S(1)}, u32[]{:S(2)}) copy-start(bf16[1,8,2,128,256]{4,3,2,1,0:T(8,128)(2,1)S(1)} %get-tuple-element.268.s_ref) | copy-start | bytes 3145732
  91.7 10.8 %copy-start.22 = (bf16[1,1024,256]{2,1,0:T(8,128)(2,1)}, bf16[1,1024,256]{2,1,0:T(8,128)(2,1)S(1)}, u32[]{:S(2)}) copy-start(bf16[1,1024,256]{2,1,0:T(8,128)(2,1)S(1)} %get-tuple-element.263) | copy-start | bytes 1572868
  91.7 10.8 %copy-start.18 = (bf16[1,8,2,128,128]{4,3,2,1,0:T(8,128)(2,1)}, bf16[1,8,2,128,128]{4,3,2,1,0:T(8,128)(2,1)S(1)}, u32[]{:S(2)}) copy-start(bf16[1,8,2,128,128]{4,3,2,1,0:T(8,128)(2,1)S(1)} %get-tuple-element.269.p_ref) | copy-start | bytes 1572868
  112.8 4.3 copy-start.41
  120.7 55.0 %copy-start.74 = (f32[1024]{0:T(1024)S(1)}, f32[1024]{0:T(1024)}, u32[]{:S(2)}) copy-start(f32[1024]{0:T(1024)} %param.39) | copy-start | bytes 12292
  120.7 121.2 %all-reduce.22.cloned.1.call-start = ((), (), s32[]{:S(2)}) async-start(), calls=%async_computation.5 | async-start | bytes 4194304 | tf_op jit(solution)/shard_map/psum | solution.py:539
  190.4 273.8 %reduce-scatter.9.cloned.1.call-start = ((), (), s32[]{:S(2)}) async-start(), calls=%async_computation.7 | async-start | bytes 1179648 | tf_op jit(solution)/shard_map/reduce_scatter | solution.py:378
  203.5 44.5 %copy-start.31 = (bf16[1,1024,1024]{2,1,0:T(8,128)(2,1)S(1)}, bf16[1,1024,1024]{2,1,0:T(8,128)(2,1)}, u32[]{:S(2)}) copy-start(bf16[1,1024,1024]{2,1,0:T(8,128)(2,1)} %param.24) | copy-start | bytes 6291460
  242.0 5.4 copy-start.86
  242.0 6.0 copy-start.36
  242.0 6.0 copy-start.50
  253.4 212.6 %reduce-scatter.7.cloned.1.call-start = ((), (), s32[]{:S(2)}) async-start(), calls=%async_computation.6 | async-start | bytes 1179648 | tf_op jit(solution)/shard_map/reduce_scatter | solution.py:378
  301.0 19.7 %copy-start.34 = (f32[1,1024,1024]{2,1,0:T(8,128)S(1)}, f32[1,1024,1024]{2,1,0:T(8,128)}, u32[]{:S(2)}) copy-start(f32[1,1024,1024]{2,1,0:T(8,128)} %copy-done.33) | copy-start | bytes 12582916
  301.0 22.0 %slice-start = ((s8[4227072]{0:T(1024)(128)(4,1)}), s8[4194304]{0:T(1024)(128)(4,1)S(1)}, s32[]{:S(2)}) async-start(s8[4227072]{0:T(1024)(128)(4,1)} %bitcast.203), calls=%async_computation.11 | async-start | bytes 8388608
  333.3 8.9 %copy-start.11 = (f32[1,2,1024,128]{3,2,1,0:T(8,128)S(1)}, f32[1,2,1024,128]{3,2,1,0:T(8,128)}, u32[]{:S(2)}) copy-start(f32[1,2,1024,128]{3,2,1,0:T(8,128)} %copy-done.10) | copy-start | bytes 3145732
  342.2 33.6 %copy-start.57 = (f32[1024,2]{1,0:T(8,128)S(1)}, f32[1024,2]{1,0:T(8,128)}, u32[]{:S(2)}) copy-start(f32[1024,2]{1,0:T(8,128)} %copy-done.56) | copy-start | bytes 24580
  342.2 33.6 %copy-start.63 = (f32[1024,2]{1,0:T(8,128)S(1)}, f32[1024,2]{1,0:T(8,128)}, u32[]{:S(2)}) copy-start(f32[1024,2]{1,0:T(8,128)} %fusion.64) | copy-start | bytes 24580
  342.2 33.6 %copy-start.117 = (f32[2]{0:T(128)S(1)}, f32[2]{0:T(128)}, u32[]{:S(2)}) copy-start(f32[2]{0:T(128)} %copy-done.116) | copy-start | bytes 28
  373.0 14.6 %collective-permute-start.1 = (bf16[1,3,1024]{2,1,0:T(4,128)(2,1)S(1)}, bf16[1,3,1024]{2,1,0:T(4,128)(2,1)S(1)}, u32[]{:S(2)}, u32[]{:S(2)}) collective-permute-start(bf16[1,3,1024]{2,1,0:T(4,128)(2,1)S(1)} %slice.261), channel_id=1, source_target_pairs={{4,0},{5,1},{6,2},{7,3},{12,8},{13,9},{14,10},{15,11},{20,16},{21,... | collective-permute-start | bytes 18440 | tf_op jit(solution)/shard_map/ppermute | solution.py:21
  387.6 152.6 %all-reduce.24.cloned.1.call-start = ((), (), s32[]{:S(2)}) async-start(), calls=%async_computation.10 | async-start | bytes 8388608 | tf_op jit(solution)/shard_map/psum | solution.py:528
  400.4 213.3 %reduce-scatter.13.cloned.1.call-start = ((), (), s32[]{:S(2)}) async-start(), calls=%async_computation.9 | async-start | bytes 2654208
  410.8 297.6 %reduce-scatter.11.cloned.1.call-start = ((), (), s32[]{:S(2)}) async-start(), calls=%async_computation.8 | async-start | bytes 5013504 | tf_op jit(solution)/shard_map/reduce_scatter | solution.py:378
  423.9 39.7 %copy-start.110 = (f32[1024]{0:T(1024)S(1)}, f32[1024]{0:T(1024)}, u32[]{:S(2)}) copy-start(f32[1024]{0:T(1024)} %get-tuple-element.455) | copy-start | bytes 12292
  423.9 116.3 %copy-start.32 = (bf16[1,1024,1024]{2,1,0:T(8,128)(2,1)S(1)}, bf16[1,1024,1024]{2,1,0:T(8,128)(2,1)}, u32[]{:S(2)}) copy-start(bf16[1,1024,1024]{2,1,0:T(8,128)(2,1)} %param.24) | copy-start | bytes 6291460
  423.9 116.3 %copy-start.73 = (f32[1024]{0:T(1024)S(1)}, f32[1024]{0:T(1024)}, u32[]{:S(2)}) copy-start(f32[1024]{0:T(1024)} %copy-done.72) | copy-start | bytes 12292
  423.9 116.3 %copy-start.95 = (f32[1024]{0:T(1024)S(1)}, f32[1024]{0:T(1024)}, u32[]{:S(2)}) copy-start(f32[1024]{0:T(1024)} %param.25) | copy-start | bytes 12292
  424.1 161.2 %copy-start.84 = (f32[1024]{0:T(1024)S(1)}, f32[1024]{0:T(1024)}, u32[]{:S(2)}) copy-start(f32[1024]{0:T(1024)} %copy-done.83) | copy-start | bytes 12292
  424.1 161.2 %copy-start.109 = (f32[1024]{0:T(1024)S(1)}, f32[1024]{0:T(1024)}, u32[]{:S(2)}) copy-start(f32[1024]{0:T(1024)} %copy-done.108) | copy-start | bytes 12292
  617.2 95.3 %copy-start.1 = (bf16[704,1024]{1,0:T(8,128)(2,1)S(1)}, bf16[704,1024]{1,0:T(8,128)(2,1)}, u32[]{:S(2)}) copy-start(bf16[704,1024]{1,0:T(8,128)(2,1)} %param.42) | copy-start | bytes 4325380
  (89 other events, 175.1 us)
Sparse Core Ops, SparseCore 0:
  120.9 51.7 all-reduce.19
  190.5 51.4 all-reduce.21
  253.5 63.7 reduce-scatter.8
  387.7 64.8 reduce-scatter.6
  455.4 84.7 all-reduce.23
  543.9 69.6 reduce-scatter.12
  617.7 90.6 reduce-scatter.10

commit v2 on v1

--- a/solution.py
+++ b/solution.py
@@ -21,28 +21,18 @@
     return lax.ppermute(value, axis, pairs)
 
 
-def entering(value, axis, combine, identity, reverse):
-    devices, index = (lax.axis_size(axis), lax.axis_index(axis))
-    everything = jax.tree.map(
-        lambda part, kind: lax.all_gather(part.astype(kind), axis),
-        value,
-        (jnp.bfloat16, jnp.bfloat16),
-    )
-    start = jax.tree.map(
-        lambda part, zero: jnp.broadcast_to(jnp.asarray(zero, part.dtype), part.shape),
-        value,
-        identity,
-    )
-
-    def lap(k, before):
-        at = devices - 1 - k if reverse else k
-        reached = at > index if reverse else at < index
-        new = combine(
-            before, jax.tree.map(lambda part, own: part[at].astype(own.dtype), everything, value)
-        )
-        return jax.tree.map(lambda a, b: jnp.where(reached, a, b), new, before)
-
-    return lax.fori_loop(0, devices, lap, start)
+def entering(carry_map, carry_add, axis, reverse):
+    devices = lax.axis_size(axis)
+    sign = -1 if reverse else 1
+    map_low, add_low = carry_map.astype(jnp.bfloat16), carry_add.astype(jnp.bfloat16)
+    state = None
+    for away in range(devices - 1, 0, -1):
+        added = shifted(add_low, axis, sign * away).astype(jnp.float32)
+        if state is None:
+            state = added
+        else:
+            state = high_dot(shifted(map_low, axis, sign * away).astype(jnp.float32), state) + added
+    return jnp.zeros_like(carry_add) if state is None else state
 
 
 def high_dot(left, right):
@@ -233,8 +223,8 @@
         q = q_ref[0, :, h * dk : (h + 1) * dk].astype(jnp.float32)
         k = k_ref[0, :, h * dk : (h + 1) * dk].astype(jnp.float32)
         v = v_ref[0, :, h * dv : (h + 1) * dv].astype(jnp.float32)
-        gate = gb_ref[0, h, :, 0:1]
-        strength = gb_ref[0, h, :, 1:2]
+        gate = gb_ref[0, :, h : h + 1]
+        strength = gb_ref[0, :, heads + h : heads + h + 1]
         decays, gammas, tails, whole = decay_parts(gate)
         lowers.append(lower_of(decays, k, strength))
         parts.append((q, k, v, strength, decays, gammas, tails, whole))
@@ -283,7 +273,7 @@
             prod[h] = jnp.where(row == col, 1.0, 0.0)
 
     for h in range(heads):
-        whole = jnp.exp(jnp.sum(gb_ref[0, h, :, 0:1], 0, keepdims=True))
+        whole = jnp.exp(jnp.sum(gb_ref[0, :, h : h + 1], 0, keepdims=True))
         now_g, now_r = total[h], prod[h]
         g_ref[0, 0, h] = now_g.astype(jnp.bfloat16)
         r_ref[0, 0, h] = now_r.astype(jnp.bfloat16)
@@ -307,12 +297,13 @@
     dq_ref, dk_ref, dv_ref, dgb_ref,
 ):
     lane = lax.broadcasted_iota(jnp.int32, (CHUNK, CHUNK), 1)
+    packed = jnp.zeros((CHUNK, CHUNK), jnp.float32)
     for h in range(heads):
         q = q_ref[0, :, h * dk : (h + 1) * dk].astype(jnp.float32)
         k = k_ref[0, :, h * dk : (h + 1) * dk].astype(jnp.float32)
         v = v_ref[0, :, h * dv : (h + 1) * dv].astype(jnp.float32)
-        gate = gb_ref[0, h, :, 0:1]
-        strength = gb_ref[0, h, :, 1:2]
+        gate = gb_ref[0, :, h : h + 1]
+        strength = gb_ref[0, :, heads + h : heads + h + 1]
         state = s_ref[0, 0, h].astype(jnp.float32) + dot_nn(p_ref[0, 0, h], in_ref[0, h])
         after = g_ref[0, 0, h].astype(jnp.float32) + dot_nn(r_ref[0, 0, h], suf_ref[0, h])
         inverse = inv_ref[0, 0, h]
@@ -323,7 +314,8 @@
         dq_ref[0, :, h * dk : (h + 1) * dk] = dq
         dk_ref[0, :, h * dk : (h + 1) * dk] = dkk
         dv_ref[0, :, h * dv : (h + 1) * dv] = dvv
-        dgb_ref[0, h] = jnp.where(lane == 0, dgate, jnp.where(lane == 1, dstrength, 0.0))
+        packed = jnp.where(lane == h, dgate, jnp.where(lane == heads + h, dstrength, packed))
+    dgb_ref[0] = packed
 
 
 def kernel_specs(heads, dk, dv, steps, reverse):
@@ -333,7 +325,7 @@
     return {
         "k": pl.BlockSpec((1, CHUNK, heads * dk), lambda s, c: (s, at(c), 0)),
         "v": pl.BlockSpec((1, CHUNK, heads * dv), lambda s, c: (s, at(c), 0)),
-        "gb": pl.BlockSpec((1, heads, CHUNK, CHUNK), lambda s, c: (s, 0, at(c), 0)),
+        "gb": pl.BlockSpec((1, CHUNK, CHUNK), lambda s, c: (s, at(c), 0)),
         "kk": pl.BlockSpec((1, 1, heads, dk, dk), lambda s, c: (s, at(c), 0, 0, 0)),
         "kv": pl.BlockSpec((1, 1, heads, dk, dv), lambda s, c: (s, at(c), 0, 0, 0)),
         "dkk": pl.BlockSpec((1, heads, dk, dk), lambda s, c: (s, 0, 0, 0)),
@@ -353,19 +345,6 @@
             dimension_semantics=("arbitrary", "arbitrary"), vmem_limit_bytes=40 * 1024 * 1024
         ),
     )
-
-
-def combine_maps(earlier, later):
-    return (high_dot(later[0], earlier[0]), high_dot(later[0], earlier[1]) + later[1])
-
-
-def identity_maps(carry_map, carry_add):
-    lane_count = carry_map.shape[0]
-    key_dim = carry_map.shape[-1]
-    eye_block = jnp.broadcast_to(
-        jnp.eye(key_dim, dtype=jnp.float32), (lane_count, key_dim, key_dim)
-    )
-    return (eye_block, jnp.zeros((lane_count,) + carry_add.shape[-2:], jnp.float32))
 
 
 def rows_dot(left, right):
@@ -438,9 +417,8 @@
             alpha_in.reshape(seq_count, local_len, heads) + bias_in
         )
         strength = jax.nn.sigmoid(beta_in.reshape(seq_count, local_len, heads))
-        both = jnp.stack([log_gate, strength], -1)
-        both = jnp.transpose(both, (0, 2, 1, 3))
-        both = jnp.pad(both, ((0, 0), (0, 0), (0, 0), (0, CHUNK - 2)))
+        both = jnp.concatenate([log_gate, strength], -1)
+        both = jnp.pad(both, ((0, 0), (0, 0), (0, CHUNK - 2 * heads)))
         return (unit_query, unit_key, raw_value, both)
 
     inputs = tokens.reshape(rows, model_width).astype(jnp.float32)
@@ -495,10 +473,8 @@
     )(queries, keys_in, values_in, both)
     device_map = device_map.reshape(lane_count, key_dim, key_dim)
     device_add = device_add.reshape(lane_count, key_dim, val_dim)
-    prefix = entering(
-        (device_map, device_add), "ctx", combine_maps, identity_maps(device_map, device_add), False
-    )
-    state_in = prefix[1].astype(low).reshape(dkv)
+    prefix = entering(device_map, device_add, "ctx", False)
+    state_in = prefix.astype(low).reshape(dkv)
     head_out = jnp.stack(
         [
             head_local[..., h * val_dim : (h + 1) * val_dim]
@@ -524,9 +500,6 @@
     hidden_f, swiglu_back = jax.vjp(swiglu, gate_pre, up_pre)
     hidden = hidden_f.astype(jnp.bfloat16)
     ffn_part = jnp.dot(hidden, down_weight, preferred_element_type=jnp.float32)
-    block_out = (
-        middle + lax.psum(ffn_part.astype(jnp.bfloat16), "tensor").astype(jnp.float32)
-    ).astype(jnp.bfloat16)
     grad_rows = cotangent.reshape(rows, model_width)
     hidden_grad = jnp.dot(grad_rows, down_weight.T, preferred_element_type=jnp.float32)
     gate_grad, up_grad = swiglu_back(hidden_grad)
@@ -541,21 +514,26 @@
     middle_grad = grad_rows.astype(jnp.float32) + middle_norm_grad
     middle_low = middle_grad.astype(jnp.bfloat16)
     ffn_cols = gate_weight.shape[1]
-    ffn_w = summed_over_rows(
-        jnp.concatenate(
-            [
-                rows_dot(normed2_b, jnp.concatenate([gate_grad_b, up_grad_b], 1)),
-                rows_dot(grad_rows, hidden),
-            ],
-            1,
-        )
-    )
+    ffn_rows = jnp.concatenate(
+        [
+            rows_dot(normed2_b, jnp.concatenate([gate_grad_b, up_grad_b], 1)),
+            rows_dot(grad_rows, hidden),
+        ],
+        1,
+    )
+    ffn_rows, ffn_low, middle_low = lax.optimization_barrier(
+        (ffn_rows, ffn_part.astype(jnp.bfloat16), middle_low)
+    )
+    ffn_sum = lax.psum(ffn_low, "tensor")
+    ffn_w = summed_over_rows(ffn_rows)
     out_w = scattered(middle_low, normed_heads_b)
     heads_grad = jnp.dot(middle_low, out_weight.T, preferred_element_type=jnp.float32).reshape(
         seq_count, local_len, heads, val_dim
     )
     head_out_grad, head_gate_gradient, head_gain_grad = gated_back(heads_grad)
     out_grad = head_out_grad.reshape(v_rows)
+    gate_lin_grad = head_gate_gradient.reshape(rows, v_cols).astype(jnp.bfloat16)
+    gate_w = scattered(normed1_b, gate_lin_grad)
     back_spec = kernel_specs(heads, key_dim, val_dim, steps, True)
     pulls, suffixes, local_pull = kernel_call(
         functools.partial(pull_kernel, heads, key_dim, val_dim, steps),
@@ -569,13 +547,9 @@
         carries,
     )(emitted, minus, both, out_grad)
     suffix = entering(
-        (flipped(device_map), local_pull.reshape(lane_count, key_dim, val_dim)),
-        "ctx",
-        combine_maps,
-        identity_maps(device_map, device_add),
-        True,
-    )
-    suffix_in = suffix[1].astype(low).reshape(dkv)
+        flipped(device_map), local_pull.reshape(lane_count, key_dim, val_dim), "ctx", True
+    )
+    suffix_in = suffix.astype(low).reshape(dkv)
     query_grad, key_grad, value_grad, both_grad = kernel_call(
         functools.partial(backward_kernel, heads, key_dim, val_dim),
         grid,
@@ -593,6 +567,9 @@
         queries, keys_in, values_in, both, inverse, states, prods,
         state_in, out_grad, pulls, suffixes, suffix_in,
     )
+    query_grad, key_grad, value_grad, both_grad, ffn_w = lax.optimization_barrier(
+        (query_grad, key_grad, value_grad, both_grad, ffn_w)
+    )
     padded_grad, kernel_grad, alpha_grad, beta_grad, decay_grad, bias_grad = front_back(
         (query_grad, key_grad, value_grad, both_grad)
     )
@@ -606,7 +583,6 @@
     query_lin_grad = linear_grad_b[:, :q_cols]
     key_lin_grad = linear_grad_b[:, q_cols : q_cols + k_cols]
     value_lin_grad = linear_grad_b[:, q_cols + k_cols :]
-    gate_lin_grad = head_gate_gradient.reshape(rows, v_cols).astype(jnp.bfloat16)
     alpha_lin_grad = alpha_grad.astype(jnp.bfloat16)
     beta_lin_grad = beta_grad.astype(jnp.bfloat16)
     paired = (
@@ -622,8 +598,11 @@
     )
     late_cols = jnp.concatenate([linear_grad_b, alpha_lin_grad, beta_lin_grad], 1)
     late_w = scattered(normed1_b, late_cols)
-    gate_w = scattered(normed1_b, gate_lin_grad)
-    normed1_grad = lax.psum(normed1_part.astype(jnp.bfloat16), "tensor").astype(jnp.float32)
+    normed1_low, ffn_sum, out_w, gate_w = lax.optimization_barrier(
+        (normed1_part.astype(jnp.bfloat16), ffn_sum, out_w, gate_w)
+    )
+    block_out = (middle + ffn_sum.astype(jnp.float32)).astype(jnp.bfloat16)
+    normed1_grad = lax.psum(normed1_low, "tensor").astype(jnp.float32)
     inputs_norm_grad, first_gain_grad = norm1_back(normed1_grad)
     tokens_grad = (middle_grad + inputs_norm_grad).astype(jnp.bfloat16)
     v_end = q_cols + k_cols + v_cols
@@ -641,13 +620,18 @@
     )
     index = lax.axis_index("tensor")
     first_own = jnp.where(index == 0, 1.0, 0.0)
-    gains = lax.psum(
-        jnp.concatenate([first_own * first_gain_grad, first_own * second_gain_grad, head_gain_grad]),
-        ("dp", "ctx", "tensor"),
-    )
-    smalls = lax.psum(
-        jnp.concatenate([kernel_grad.reshape(-1), decay_grad, bias_grad]), ("dp", "ctx")
-    )
+    gains = jnp.sum(
+        lax.all_gather(
+            jnp.concatenate(
+                [first_own * first_gain_grad, first_own * second_gain_grad, head_gain_grad]
+            ),
+            ("dp", "ctx", "tensor"),
+        ),
+        0,
+    )
+    own = jnp.concatenate([kernel_grad.reshape(-1), decay_grad, bias_grad])
+    own = jnp.pad(own, (0, -own.size % 1024))
+    smalls = jnp.sum(lax.all_gather(own, ("dp", "ctx")), 0)
     taps = kernel_grad.size
     small_sums = (
         gains[:model_width],
@@ -655,7 +639,7 @@
         gains[2 * model_width :],
         smalls[:taps].reshape(kernel_grad.shape),
         smalls[taps : taps + heads],
-        smalls[taps + heads :],
+        smalls[taps + heads : taps + 2 * heads],
     )
     kernel_sum = small_sums[3]
     return (

time: 730 us -> 658 us (0.901)
  blocking collectives: 102 us -> 72.9 us
  local copies, waits for them, and re-layouts: 112 us -> 88.1 us
  matrix products: 81.6 us -> 67.1 us
    psum x2 -> x0, blocking collectives: 78.8 us -> none  [the longest x1 40.5 us: per_device(): lax.psum(jnp.concatenate([first_own * first_gain_grad, first_own * second...]
    psum x1 -> x2, waiting for transfers between devices: 72.6 us -> 12.3 us  [the longest x1 11.2 us: per_device(): ffn_sum = lax.psum(ffn_low, 'tensor')]
    reduce_scatter x3, waiting for transfers between devices: 90.6 us -> 148 us  [summed_over_rows(): lax.psum_scatter(partial, ('dp', 'ctx'), scatter_dimension=0, tiled=True)]
    all_gather x4 -> x2, blocking collectives: 23.3 us -> 72.9 us  [the longest x1 42.2 us: per_device(): lax.all_gather(jnp.concatenate([first_own * first_gain_grad, first_own *...]
    pallas_call x1 -> x0, local copies, waits for them, and re-layouts: 30 us -> none  [per_device(): kernel_call(functools.partial(backward_kernel, heads, key_dim, val_dim),...]
    unnamed x273 -> x292, local copies, waits for them, and re-layouts: 37.8 us -> 61.1 us
    another operation x2 -> x0, local copies, waits for them, and re-layouts: 16.2 us -> none  [mixer_front(): both = jnp.stack([log_gate, strength], -1)]
    unnamed x8 -> x9, waiting for transfers between devices: 21.1 us -> 19 us
  transfers between devices with their start and end apart: 9 -> 12, of which waited for: 5 -> 9; matrix products, arithmetic and copies ran while one was open for 25% -> 18% of each run, Pallas kernels for 3% -> 4%
where the time goes in v2:
time: 658 us; the launch traced here: 648 us
  waiting for transfers between devices  273 us (41%)
  local copies, waits for them, and re-layouts  88.1 us (13%)
  blocking collectives  72.9 us (11%)
  other arithmetic  70.4 us (11%)
  matrix products  67.1 us (10%)
  Pallas kernels  50.2 us (8%)
  between operations  15.9 us (2%)
  starting transfers between devices  10.1 us (2%)
    reduce_scatter x3, waiting for transfers between devices, summed_over_rows(): lax.psum_scatter(partial, ('dp', 'ctx'), scatter_dimension=0, tiled=True)  148 us
    unnamed x292, local copies, waits for them, and re-layouts  61.1 us
    psum x1, waiting for transfers between devices, per_device(): lax.psum(mixer_part.astype(jnp.bfloat16), 'tensor').astype(jnp.float32)  45 us
    psum x1, waiting for transfers between devices, per_device(): lax.psum(normed2_part.astype(jnp.bfloat16), 'tensor').astype(jnp.float32)  43.4 us
    all_gather x1, blocking collectives, per_device(): lax.all_gather(jnp.concatenate([first_own * first_gain_grad, first_own *...  42.2 us
    all_gather x1, blocking collectives, per_device(): smalls = jnp.sum(lax.all_gather(own, ('dp', 'ctx')), 0)  30.6 us
    pallas_call x1, Pallas kernels, per_device(): kernel_call(functools.partial(forward_kernel, heads, key_dim, val_dim, st...  27 us
    pallas_call x1, Pallas kernels, per_device(): kernel_call(functools.partial(backward_kernel, heads, key_dim, val_dim),...  19.3 us
  transfers between devices with their start and end apart: 12, of which 9 were waited for; matrix products, arithmetic and copies ran while one was open for 18% of the time, Pallas kernels for 4%

profile of v2, /device:TPU:0, one launch (start us, length us, event | category | flops | bytes accessed | tf_op | source)
XLA Modules:
  0.0 647.9 jit_solution(9195870325361804021)
XLA Ops:
  7.3 2.2 fusion.13
  15.9 5.0 collective-permute-start
  22.4 2.7 fusion.82
  27.3 3.9 fusion.16
  34.0 27.0 %shard_map.347 = (bf16[1,1024,256]{2,1,0:T(8,128)(2,1)S(1)}, bf16[1,1024,256]{2,1,0:T(8,128)(2,1)S(1)}, f32[1,1024,512]{2,1,0:T(8,128)S(1)}, bf16[1,8,2,128,128]...) custom-call(bf16[1,1024,256]{2,1,0:T(8,128)(2,1)S(1)} %fusion.50.q_r, ...), custom_call_target="tpu_custom_call" | custom-call | tf_op jit(solution)/shard_map/pallas_call | solution.py:457
  69.2 2.9 copy.152
  86.5 2.6 convolution_convert_fusion.2
  89.2 2.9 copy.156
  92.0 5.2 fusion.33
  97.3 45.0 %all-reduce.21.cloned.1.call-done = bf16[1024,1024]{1,0:T(8,128)(2,1)} async-done(((bf16[1024,1024]{1,0:T(8,128)(2,1)}), bf16[1024,1024]{1,0:T(8,128)(2,1)}) %all-reduce.21.cloned.1.call-update) | async-done | bytes 2097168 | tf_op jit(solution)/shard_map/psum | solution.py:495
  142.3 3.1 multiply_reduce_fusion.4
  149.7 4.3 fusion.19
  154.1 2.8 fusion.39
  156.8 3.2 convolution_convert_fusion.3
  160.1 2.7 copy.153
  162.8 3.4 fusion.84
  166.2 3.3 add_convert_fusion.2
  169.6 5.7 convolution_convert_fusion.1
  175.3 2.4 pad_maximum_fusion
  177.7 43.4 %all-reduce.23.cloned.1.call-done = bf16[1024,1024]{1,0:T(8,128)(2,1)} async-done(((bf16[1024,1024]{1,0:T(8,128)(2,1)}), bf16[1024,1024]{1,0:T(8,128)(2,1)}) %all-reduce.23.cloned.1.call-update) | async-done | bytes 2097168 | tf_op jit(solution)/shard_map/psum | solution.py:512
  221.1 4.7 fusion.6
  229.1 2.2 convolution_convert_fusion.5
  231.4 3.1 fusion.85
  237.8 3.1 copy.157
  240.9 3.0 multiply_reduce_fusion.6
  247.8 4.1 multiply_reduce_fusion.5
  252.9 2.3 convolution_convert_fusion.4
  259.0 3.9 shard_map.348
  266.0 3.3 fusion.86
  269.4 3.0 collective-permute-done.2
  281.1 19.3 %shard_map.349 = (f32[1,1024,256]{2,1,0:T(8,128)S(1)}, f32[1,1024,256]{2,1,0:T(8,128)S(1)}, f32[1,1024,512]{2,1,0:T(8,128)S(1)}, f32[1,1024,128]{2,1,0:T(8,128)S(1)}) custom-call(bf16[1,1024,256]{2,1,0:T(8,128)(2,1)S(1)} %copy-done.6, bf16[1,1024,256]{2,1,0:T(8,128)(2,1)S(1)} %copy-done.8, bf16[1,1024,512]{2,1,0:T(8,128)(2,1)S(1)} %slice.270.v_ref, ...), custom_call_target="tpu_custom_call" | custom-call | tf_op jit(solution)/shard_map/pallas_call | solution.py:553
  306.3 55.0 %reduce-scatter.11.cloned.1.call-done = bf16[128,512]{1,0:T(8,128)(2,1)} async-done(((bf16[1024,512]{1,0:T(8,128)(2,1)}), bf16[128,512]{1,0:T(8,128)(2,1)}) %reduce-scatter.11.cloned.1.call-update) | async-done | bytes 131088 | tf_op jit(solution)/shard_map/reduce_scatter | solution.py:357
  362.9 92.5 %reduce-scatter.7.cloned.1.call-done = bf16[128,2112]{1,0:T(8,128)(2,1)} async-done(((bf16[1024,2112]{1,0:T(8,128)(2,1)}), bf16[128,2112]{1,0:T(8,128)(2,1)}) %reduce-scatter.7.cloned.1.call-update) | async-done | bytes 540688 | tf_op jit(solution)/shard_map/reduce_scatter | solution.py:357
  458.4 2.8 fusion.87
  466.5 3.4 multiply_reduce_fusion.3
  470.0 5.2 broadcast_multiply_fusion
  475.2 6.9 %pad_add_fusion = f32[1,1027,1024]{2,1,0:T(8,128)S(1)} fusion(f32[1,1024,1024]{2,1,0:T(8,128)} %get-tuple-element.212, f32[1,1024,1024]{2,1,0:T(8,128)} %get-tuple-element.213, f32[1,1024,1024]{2,1,0:T(8,128)} %get-tuple-element.214, f32[1,1024,1024]{2,1,0:T(8,128)S(1)} %get-tuple-element.211), kind=kLoop, calls=%fused_computation.18 | loop fusion | flops 3154944 | bytes 20983808 | tf_op jit(solution)/shard_map/transpose(jvp())/add_any | solution.py:402
  484.5 3.1 collective-permute-done.3
  492.0 5.7 add_convert_fusion.1
  497.7 11.2 %all-reduce.25.cloned.1.call-done = bf16[1024,1024]{1,0:T(8,128)(2,1)} async-done(((bf16[1024,1024]{1,0:T(8,128)(2,1)}), bf16[1024,1024]{1,0:T(8,128)(2,1)}) %all-reduce.25.cloned.1.call-update) | async-done | bytes 2097168 | tf_op jit(solution)/shard_map/psum | solution.py:527
  509.0 3.1 concatenate.120
  512.1 4.7 convolution_convert_fusion
  516.8 2.5 copy.176
  520.7 30.6 %all-gather.1 = f32[40960]{0:T(1024)S(1)} all-gather(f32[5120]{0:T(1024)S(1)} %pad.73), channel_id=3, replica_groups=mesh['dp'=4,'ctx'=2,'tensor'=4] {'dp','ctx'}, dimensions={0}, use_global_device_ids=true | all-gather | bytes 184320 | tf_op jit(solution)/shard_map/all_gather | solution.py:634
  563.3 3.3 fusion.7
  566.7 42.2 %all-gather.2 = f32[32,1,2304]{2,1,0:T(1,128)S(1)} all-gather(f32[1,1,2304]{2,1,0:T(1,128)S(1)} %reshape.750), channel_id=2, replica_groups=mesh['dp'=4,'ctx'=2,'tensor'=4] {'dp','ctx','tensor'}, dimensions={0}, use_global_device_ids=true | all-gather | bytes 304128 | tf_op jit(solution)/shard_map/all_gather | solution.py:624
  610.3 8.1 %fusion.30 = (bf16[1,1024,1024]{2,1,0:T(8,128)(2,1)}, bf16[1,1024,1024]{2,1,0:T(8,128)(2,1)}) fusion(bf16[1024,1024]{1,0:T(8,128)(2,1)} %all-reduce.27.cloned.1.call-done, bf16[1,1024,1024]{2,1,0:T(8,128)(2,1)S(1)} %copy-done.39, f32[1024]{0:T(1024)S(1)} %multiply_multiply_fusion.1, f32[1024]{0:T(1024)} %param.21, f32[1024]{0:T(1024)S(1)} %copy-done.85, ...), kind=kLoop, calls=%fused_computation.65 | loop fusion | flops 23068672 | bytes 16801792 | tf_op jit(solution)/shard_map/reshape | solution.py:647
  618.4 18.3 %reduce-scatter.13.cloned.1.call-done = bf16[128,1028]{1,0:T(8,128)(2,1)} async-done(((bf16[1024,1028]{1,0:T(8,128)(2,1)}), bf16[128,1028]{1,0:T(8,128)(2,1)}) %reduce-scatter.13.cloned.1.call-update) | async-done | bytes 263184
  (396 shorter events, 107.6 us)
Async XLA Ops:
  7.2 141.7 %copy-start = (bf16[1024,704]{0,1:T(8,128)(2,1)S(1)}, bf16[1024,704]{0,1:T(8,128)(2,1)}, u32[]{:S(2)}) copy-start(bf16[1024,704]{0,1:T(8,128)(2,1)} %param.36) | copy-start | bytes 4325380
  7.2 135.1 %all-reduce.21.cloned.1.call-start = ((), (), s32[]{:S(2)}) async-start(), calls=%async_computation.4 | async-start | bytes 4194304 | tf_op jit(solution)/shard_map/psum | solution.py:495
  11.9 13.2 %copy-start.59 = (bf16[1024,1024]{1,0:T(8,128)(2,1)}, bf16[1024,1024]{1,0:T(8,128)(2,1)S(1)}, u32[]{:S(2)}) copy-start(bf16[1024,1024]{1,0:T(8,128)(2,1)S(1)} %fusion.4) | copy-start | bytes 6291460
  15.8 5.3 copy-start.132
  15.9 5.4 copy-start.119
  15.9 5.4 copy-start.120
  15.9 5.4 copy-start.116
  15.9 5.4 copy-start.117
  15.9 10.7 %collective-permute-start = (bf16[1,3,1024]{2,1,0:T(4,128)(2,1)S(1)}, bf16[1,3,1024]{2,1,0:T(4,128)(2,1)S(1)}, u32[]{:S(2)}, u32[]{:S(2)}) collective-permute-start(bf16[1,3,1024]{2,1,0:T(4,128)(2,1)S(1)} %pad_maximum_fusion.4), channel_id=1, source_target_pairs={{0,4},{1,5},{2,6},{3,7},{8,12},{9,13},{10,14},{11,15},{16,20},{17,... | collective-permute-start | bytes 18440 | tf_op jit(solution)/shard_map/ppermute | solution.py:21
  21.3 5.9 copy-start.103
  21.3 5.9 copy-start.105
  21.3 5.9 copy-start.107
  21.4 5.9 copy-start.109
  26.6 7.4 %copy-start.2 = (f32[1,1024,128]{2,1,0:T(8,128)}, f32[1,1024,128]{2,1,0:T(8,128)S(1)}, u32[]{:S(2)}) copy-start(f32[1,1024,128]{2,1,0:T(8,128)S(1)} %select_maximum_fusion.gb_ref) | copy-start | bytes 1572868
  33.9 32.2 %copy-start.7 = (bf16[1,1024,256]{2,1,0:T(8,128)(2,1)}, bf16[1,1024,256]{2,1,0:T(8,128)(2,1)S(1)}, u32[]{:S(2)}) copy-start(bf16[1,1024,256]{2,1,0:T(8,128)(2,1)S(1)} %pad_maximum_fusion.2.k_ref) | copy-start | bytes 1572868
  33.9 35.3 %copy-start.122 = (f32[256]{0:T(256)S(1)}, f32[256]{0:T(256)}, u32[]{:S(2)}) copy-start(f32[256]{0:T(256)} %param.33) | copy-start | bytes 3076
  34.0 27.1 %copy-start.5 = (bf16[1,1024,256]{2,1,0:T(8,128)(2,1)}, bf16[1,1024,256]{2,1,0:T(8,128)(2,1)S(1)}, u32[]{:S(2)}) copy-start(bf16[1,1024,256]{2,1,0:T(8,128)(2,1)S(1)} %fusion.50.q_ref) | copy-start | bytes 1572868
  66.1 6.0 copy-start.34
  67.4 4.7 collective-permute-start.1
  89.1 132.0 %all-reduce.23.cloned.1.call-start = ((), (), s32[]{:S(2)}) async-start(), calls=%async_computation.5 | async-start | bytes 4194304 | tf_op jit(solution)/shard_map/psum | solution.py:512
  97.3 48.2 %copy-start.83 = (f32[1024]{0:T(1024)S(1)}, f32[1024]{0:T(1024)}, u32[]{:S(2)}) copy-start(f32[1024]{0:T(1024)} %param.35) | copy-start | bytes 12292
  169.5 135.0 %reduce-scatter.9.cloned.1.call-start = ((), (), s32[]{:S(2)}) async-start(), calls=%async_computation.8 | async-start | bytes 1179648 | tf_op jit(solution)/shard_map/reduce_scatter | solution.py:357
  169.6 5.7 copy-start.62
  175.3 45.8 %copy-start.38 = (bf16[1,1024,1024]{2,1,0:T(8,128)(2,1)S(1)}, bf16[1,1024,1024]{2,1,0:T(8,128)(2,1)}, u32[]{:S(2)}) copy-start(bf16[1,1024,1024]{2,1,0:T(8,128)(2,1)} %param.20) | copy-start | bytes 6291460
  231.3 129.9 %reduce-scatter.11.cloned.1.call-start = ((), (), s32[]{:S(2)}) async-start(), calls=%async_computation.9 | async-start | bytes 1179648 | tf_op jit(solution)/shard_map/reduce_scatter | solution.py:357
  255.2 200.2 %reduce-scatter.7.cloned.1.call-start = ((), (), s32[]{:S(2)}) async-start(), calls=%async_computation.6 | async-start | bytes 5013504 | tf_op jit(solution)/shard_map/reduce_scatter | solution.py:357
  255.8 253.1 %all-reduce.25.cloned.1.call-start = ((), (), s32[]{:S(2)}) async-start(), calls=%async_computation.7 | async-start | bytes 4194304 | tf_op jit(solution)/shard_map/psum | solution.py:527
  259.0 7.0 %copy-start.76 = (bf16[1024,512]{1,0:T(8,128)(2,1)S(1)}, bf16[1024,512]{1,0:T(8,128)(2,1)}, u32[]{:S(2)}) copy-start(bf16[1024,512]{1,0:T(8,128)(2,1)} %copy-done.75) | copy-start | bytes 3145732
  259.0 7.0 %copy-start.131 = (bf16[1024,512]{1,0:T(8,128)(2,1)S(1)}, bf16[1024,512]{1,0:T(8,128)(2,1)}, u32[]{:S(2)}) copy-start(bf16[1024,512]{1,0:T(8,128)(2,1)} %param.25) | copy-start | bytes 3145732
  264.7 7.7 %collective-permute-start.2 = (bf16[2,128,256]{2,1,0:T(8,128)(2,1)S(1)}, bf16[2,128,256]{2,1,0:T(8,128)(2,1)S(1)}, u32[]{:S(2)}, u32[]{:S(2)}) collective-permute-start(bf16[2,128,256]{2,1,0:T(8,128)(2,1)S(1)} %convert_bitcast_fusion.1), channel_id=1, source_target_pairs={{4,0},{5,1},{6,2},{7,3},{12,8},{13,9},{14,10},{15,11},{20,16},{21,... | collective-permute-start | bytes 393224 | tf_op jit(solution)/shard_map/ppermute | solution.py:21
  269.3 294.0 %all-reduce.27.cloned.1.call-start = ((), (), s32[]{:S(2)}) async-start(), calls=%async_computation.10 | async-start | bytes 4194304 | tf_op jit(solution)/shard_map/psum | solution.py:605
  304.5 153.0 %copy-start.65 = (f32[1024,2]{1,0:T(8,128)S(1)}, f32[1024,2]{1,0:T(8,128)}, u32[]{:S(2)}) copy-start(f32[1024,2]{1,0:T(8,128)} %copy-done.64) | copy-start | bytes 24580
  304.5 153.0 %copy-start.69 = (f32[1024,2]{1,0:T(8,128)S(1)}, f32[1024,2]{1,0:T(8,128)}, u32[]{:S(2)}) copy-start(f32[1024,2]{1,0:T(8,128)} %copy-done.68) | copy-start | bytes 24580
  304.5 153.0 %copy-start.124 = (f32[2]{0:T(128)S(1)}, f32[2]{0:T(128)}, u32[]{:S(2)}) copy-start(f32[2]{0:T(128)} %copy-done.123) | copy-start | bytes 28
  304.5 153.0 %copy-start.16 = (f32[1,1024,128]{2,1,0:T(8,128)S(1)}, f32[1,1024,128]{2,1,0:T(8,128)}, u32[]{:S(2)}) copy-start(f32[1,1024,128]{2,1,0:T(8,128)} %copy-done.15) | copy-start | bytes 1572868
  306.2 152.0 %copy-start.22 = (f32[1,1024,256]{2,1,0:T(8,128)S(1)}, f32[1,1024,256]{2,1,0:T(8,128)}, u32[]{:S(2)}) copy-start(f32[1,1024,256]{2,1,0:T(8,128)} %copy-done.21) | copy-start | bytes 3145732
  458.3 6.8 %slice-start = ((s8[4227072]{0:T(1024)(128)(4,1)}), s8[4194304]{0:T(1024)(128)(4,1)S(1)}, s32[]{:S(2)}) async-start(s8[4227072]{0:T(1024)(128)(4,1)} %bitcast.186), calls=%async_computation.12 | async-start | bytes 8388608
  475.2 8.7 %copy-start.118 = (bf16[1024,2]{0,1:T(2,128)(2,1)S(1)}, bf16[1024,2]{0,1:T(2,128)(2,1)}, u32[]{:S(2)}) copy-start(bf16[1024,2]{0,1:T(2,128)(2,1)} %param.27) | copy-start | bytes 12292
  482.1 5.5 collective-permute-start.3
  508.9 127.8 %reduce-scatter.13.cloned.1.call-start = ((), (), s32[]{:S(2)}) async-start(), calls=%async_computation.11 | async-start | bytes 2654208
  519.3 33.3 %copy-start.63 = (f32[128,2112]{1,0:T(8,128)S(1)}, f32[128,2112]{1,0:T(8,128)}, u32[]{:S(2)}) copy-start(f32[128,2112]{1,0:T(8,128)} %convert_element_type.190) | copy-start | bytes 3244036
  551.4 10.0 %copy-start.77 = (f32[128,512]{1,0:T(8,128)S(1)}, f32[128,512]{1,0:T(8,128)}, u32[]{:S(2)}) copy-start(f32[128,512]{1,0:T(8,128)} %convert_element_type.200) | copy-start | bytes 786436
  552.6 10.7 %copy-start.39 = (bf16[1,1024,1024]{2,1,0:T(8,128)(2,1)S(1)}, bf16[1,1024,1024]{2,1,0:T(8,128)(2,1)}, u32[]{:S(2)}) copy-start(bf16[1,1024,1024]{2,1,0:T(8,128)(2,1)} %param.20) | copy-start | bytes 6291460
  552.6 10.7 %copy-start.85 = (f32[1024]{0:T(1024)S(1)}, f32[1024]{0:T(1024)}, u32[]{:S(2)}) copy-start(f32[1024]{0:T(1024)} %copy-done.84) | copy-start | bytes 12292
  552.6 10.7 %copy-start.102 = (f32[1024]{0:T(1024)S(1)}, f32[1024]{0:T(1024)}, u32[]{:S(2)}) copy-start(f32[1024]{0:T(1024)} %param.21) | copy-start | bytes 12292
  561.4 5.2 copy-start.121
  562.3 48.0 %copy-start.93 = (f32[1024]{0:T(1024)S(1)}, f32[1024]{0:T(1024)}, u32[]{:S(2)}) copy-start(f32[1024]{0:T(1024)} %copy-done.92) | copy-start | bytes 12292
  610.3 30.6 %copy-start.1 = (bf16[1024,704]{0,1:T(8,128)(2,1)S(1)}, bf16[1024,704]{0,1:T(8,128)(2,1)}, u32[]{:S(2)}) copy-start(bf16[1024,704]{0,1:T(8,128)(2,1)} %param.36) | copy-start | bytes 4325380
  (101 other events, 210.0 us)
Sparse Core Ops, SparseCore 0:
  89.2 53.0 all-reduce.20
  169.6 51.4 all-reduce.22
  231.5 63.6 reduce-scatter.8
  298.8 62.3 reduce-scatter.10
  364.7 90.6 reduce-scatter.6
  457.7 51.1 all-reduce.24
  511.9 51.4 all-reduce.26
  567.2 69.4 reduce-scatter.12
